TPU v7x, 32 devices: a whole 2x2x4 slice. The times are simulated.
32 devices in a mesh: seq: 16 (over z, y, x), rep: 2 (over core).
Axes of the slice: x: 2, y: 2, z: 4, core: 2. Of those that a mesh axis runs over, the one named last changes fastest.
Arguments:
- tokens: bfloat16 [16, 2, 1024, 768], P('rep', None, 'seq'), may hold values from -6 to 6
- mixer_gain: bfloat16 [768], P(('seq', 'rep')), may hold values from 0.5 to 1.5
- mixer_bias: bfloat16 [768], P(('seq', 'rep')), may hold values from -1.75 to 1.75
- key_blend: bfloat16 [768], P(('seq', 'rep')), may hold values from 0.019897461 to 0.3984375
- value_blend: bfloat16 [768], P(('seq', 'rep')), may hold values from 0.019897461 to 0.3984375
- gate_blend: bfloat16 [768], P(('seq', 'rep')), may hold values from 0.019897461 to 0.3984375
- time_decay: bfloat16 [768], P(('seq', 'rep')), may hold values from -10 to -2.796875
- time_first: bfloat16 [768], P(('seq', 'rep')), may hold values from -1 to 1
- key_weight: bfloat16 [768, 768], P(('seq', 'rep')), may hold values from -0.21875 to 0.21875
- value_weight: bfloat16 [768, 768], P(('seq', 'rep')), may hold values from -0.875 to 0.875
- gate_weight: bfloat16 [768, 768], P(('seq', 'rep')), may hold values from -0.21875 to 0.21875
- output_weight: bfloat16 [768, 768], P(('seq', 'rep')), may hold values from -0.875 to 0.875
- channel_gain: bfloat16 [768], P(('seq', 'rep')), may hold values from 0.5 to 1.5
- channel_bias: bfloat16 [768], P(('seq', 'rep')), may hold values from -1.75 to 1.75
- hidden_blend: bfloat16 [768], P(('seq', 'rep')), may hold values from 0.049804688 to 0.94921875
- screen_blend: bfloat16 [768], P(('seq', 'rep')), may hold values from 0.049804688 to 0.94921875
- hidden_weight: bfloat16 [768, 3072], P(('seq', 'rep')), may hold values from -0.21875 to 0.21875
- screen_weight: bfloat16 [768, 768], P(('seq', 'rep')), may hold values from -0.21875 to 0.21875
- return_weight: bfloat16 [3072, 768], P(('seq', 'rep')), may hold values from -0.109375 to 0.109375
- cotangent: bfloat16 [16, 2, 1024, 768], P('rep', None, 'seq'), may hold values from -6 to 6
Outputs:
- output: bfloat16 [16, 2, 1024, 768], P('rep', None, 'seq')
- input_grad: float32 [16, 2, 1024, 768], P('rep', None, 'seq')
- final_numerator: float32 [16, 768], P('rep', 'seq')
- final_denominator: float32 [16, 768], P('rep', 'seq')
- final_maximum: float32 [16, 768], P('rep', 'seq')
- mixer_gain_grad: float32 [768], P(('seq', 'rep'))
- mixer_bias_grad: float32 [768], P(('seq', 'rep'))
- key_blend_grad: float32 [768], P(('seq', 'rep'))
- value_blend_grad: float32 [768], P(('seq', 'rep'))
- gate_blend_grad: float32 [768], P(('seq', 'rep'))
- time_decay_grad: float32 [768], P(('seq', 'rep'))
- time_first_gradient: float32 [768], P(('seq', 'rep'))
- key_weight_grad: float32 [768, 768], P(('seq', 'rep'))
- value_weight_grad: float32 [768, 768], P(('seq', 'rep'))
- gate_weight_grad: float32 [768, 768], P(('seq', 'rep'))
- output_weight_grad: float32 [768, 768], P(('seq', 'rep'))
- channel_gain_grad: float32 [768], P(('seq', 'rep'))
- channel_bias_grad: float32 [768], P(('seq', 'rep'))
- hidden_blend_grad: float32 [768], P(('seq', 'rep'))
- screen_blend_grad: float32 [768], P(('seq', 'rep'))
- hidden_weight_grad: float32 [768, 3072], P(('seq', 'rep'))
- screen_weight_grad: float32 [768, 768], P(('seq', 'rep'))
- return_weight_grad: float32 [3072, 768], P(('seq', 'rep'))
All inputs are finite; a program needn't handle non-finite values.
Results may differ from a plain program's by a relative error of at most 0.012.
Values may be sent and summed in bfloat16 or wider, within the bound.
A program may use at most 320 MiB of HBM per device.

v0:
```python
import math

import jax
import jax.numpy as jnp
from jax import lax
from jax.sharding import PartitionSpec as P

highest = lax.Precision.HIGHEST
norm_eps = 1e-05


def from_behind(value, axis, steps):
    count = lax.axis_size(axis)
    pairs = [(source, (source + steps) % count) for source in range(count)]
    return lax.ppermute(value, axis, pairs)


def norm_rows(values, norm_gain, norm_bias):
    centred = values - jnp.mean(values, -1, keepdims=True)
    inverse = lax.rsqrt(jnp.mean(centred * centred, -1, keepdims=True) + norm_eps)
    scaled = centred * inverse
    return (scaled * norm_gain + norm_bias, scaled, inverse)


def norm_back(upstream, scaled, inverse, norm_gain):
    inner_quantity = upstream * norm_gain
    centred = inner_quantity - jnp.mean(inner_quantity, -1, keepdims=True)
    return inverse * (centred - scaled * jnp.mean(inner_quantity * scaled, -1, keepdims=True))


def product(operand, matrix):
    flattened = operand.reshape(-1, operand.shape[-1])
    result = jnp.dot(flattened, matrix, preferred_element_type=jnp.float32)
    return result.reshape(operand.shape[:-1] + (matrix.shape[-1],))


def product_back(upstream, matrix):
    flattened = upstream.reshape(-1, upstream.shape[-1])
    result = lax.dot_general(
        flattened, matrix, (((1,), (1,)), ((), ())), preferred_element_type=jnp.float32
    )
    return result.reshape(upstream.shape[:-1] + (matrix.shape[0],))


def weight_grad(operand, upstream):
    flat_left = operand.reshape(-1, operand.shape[-1])
    flat_right = upstream.reshape(-1, upstream.shape[-1])
    return lax.dot_general(
        flat_left, flat_right, (((0,), (0,)), ((), ())), preferred_element_type=jnp.float32
    )


def blend(current_element, before, portion):
    return before + (current_element - before) * portion


def decay_tables(fading_multiplier, block_size, block_count):
    offsets = jnp.arange(block_size, dtype=jnp.float32)
    spacing = offsets[:, None] - 1.0 - offsets[None, :]
    within = jnp.where(
        spacing[:, :, None] >= 0.0,
        jnp.exp(-jnp.maximum(spacing, 0.0)[:, :, None] * fading_multiplier),
        0.0,
    )
    leading = jnp.exp(-offsets[:, None] * fading_multiplier)
    trailing = jnp.exp(-(block_size - 1.0 - offsets)[:, None] * fading_multiplier)
    block_index = jnp.arange(block_count, dtype=jnp.float32)
    distance = block_index[:, None] - 1.0 - block_index[None, :]
    stride_rate = block_size * fading_multiplier
    across = jnp.where(
        distance[:, :, None] >= 0.0,
        jnp.exp(-jnp.maximum(distance, 0.0)[:, :, None] * stride_rate),
        0.0,
    )
    opening = jnp.exp(-block_index[:, None] * stride_rate)
    closing = jnp.exp(-(block_count - 1.0 - block_index)[:, None] * stride_rate)
    return (within, leading, trailing, across, opening, closing)


def einsum_texts():
    return (
        "tic,...cmi->...cmt",
        "ic,...cmi->...cm",
        "mc,...cm->...c",
        "jmc,...cm->...cj",
        "tic,...cmt->...cmi",
        "tc,...cmt->...cm",
        "mc,...cm->...c",
        "jmc,...cj->...cm",
    )


def to_blocks(stacked, block_size):
    layout = stacked.shape
    return stacked.reshape(layout[:-1] + (layout[-1] // block_size, block_size))


def per_feature_mode(vector):
    return vector[:, None]


def wkv_prepare(address_matrix_tile, payload_matrix_tile, fading_multiplier, block_size):
    length = address_matrix_tile.shape[-1]
    precomputed_exponentials = decay_tables(fading_multiplier, block_size, length // block_size)
    within, leading, trailing, across, opening, closing = precomputed_exponentials
    texts = einsum_texts()
    expansion_ratio = jnp.exp(address_matrix_tile)
    blocked = to_blocks(
        jnp.stack([expansion_ratio * payload_matrix_tile, expansion_ratio]), block_size
    )
    inner_quantity = jnp.einsum(texts[0], within, blocked, precision=highest)
    cumulative_sums = jnp.einsum(texts[1], trailing, blocked, precision=highest)
    aggregate_result = jnp.einsum(texts[2], closing, cumulative_sums, precision=highest)
    return (precomputed_exponentials, inner_quantity, cumulative_sums, aggregate_result)


def weighted_value_complete(
    address_matrix_tile,
    payload_matrix_tile,
    temporal_reward_exponent,
    precomputed_exponentials,
    inner_quantity,
    cumulative_sums,
    inbound_state,
):
    within, leading, trailing, across, opening, closing = precomputed_exponentials
    texts = einsum_texts()
    arrival = jnp.einsum(texts[3], across, cumulative_sums, precision=highest)
    carried_snapshots = (
        inner_quantity
        + jnp.transpose(leading)[:, None, :]
        * (arrival + jnp.transpose(opening) * inbound_state[..., :, None])[..., None]
    )
    carried_snapshots = carried_snapshots.reshape((2,) + address_matrix_tile.shape)
    reward_scaled_entry = jnp.exp(per_feature_mode(temporal_reward_exponent) + address_matrix_tile)
    blended_input = (carried_snapshots[0] + reward_scaled_entry * payload_matrix_tile) / (
        carried_snapshots[1] + reward_scaled_entry
    )
    return (blended_input, carried_snapshots)


def weighted_value_gradient_setup(
    arriving_entries,
    address_matrix_tile,
    payload_matrix_tile,
    temporal_reward_exponent,
    carried_snapshots,
    precomputed_exponentials,
):
    within, leading, trailing, across, opening, closing = precomputed_exponentials
    texts = einsum_texts()
    reward_scaled_entry = jnp.exp(per_feature_mode(temporal_reward_exponent) + address_matrix_tile)
    normalizer_sum = carried_snapshots[1] + reward_scaled_entry
    dividend_adjoint_sum = arriving_entries / normalizer_sum
    divisor_adjoint_sum = (
        -dividend_adjoint_sum
        * (carried_snapshots[0] + reward_scaled_entry * payload_matrix_tile)
        / normalizer_sum
    )
    blocked = to_blocks(jnp.stack([dividend_adjoint_sum, divisor_adjoint_sum]), within.shape[0])
    inner_quantity = jnp.einsum(texts[4], within, blocked, precision=highest)
    cumulative_sums = jnp.einsum(texts[5], leading, blocked, precision=highest)
    aggregate_result = jnp.einsum(texts[6], opening, cumulative_sums, precision=highest)
    return (
        dividend_adjoint_sum,
        divisor_adjoint_sum,
        reward_scaled_entry,
        inner_quantity,
        cumulative_sums,
        aggregate_result,
    )


def weighted_value_gradient_complete(
    address_matrix_tile,
    payload_matrix_tile,
    fading_multiplier,
    dividend_adjoint_sum,
    divisor_adjoint_sum,
    reward_scaled_entry,
    carried_snapshots,
    precomputed_exponentials,
    inner_quantity,
    cumulative_sums,
    leaving,
):
    within, leading, trailing, across, opening, closing = precomputed_exponentials
    texts = einsum_texts()
    arrival = jnp.einsum(texts[7], across, cumulative_sums, precision=highest)
    cotangent_seed = (
        inner_quantity
        + jnp.transpose(trailing)[:, None, :]
        * (arrival + jnp.transpose(closing) * leaving[..., :, None])[..., None]
    )
    cotangent_seed = cotangent_seed.reshape(carried_snapshots.shape)
    expansion_ratio = jnp.exp(address_matrix_tile)
    current_element = payload_matrix_tile * dividend_adjoint_sum + divisor_adjoint_sum
    address_derivative = (
        expansion_ratio * (payload_matrix_tile * cotangent_seed[0] + cotangent_seed[1])
        + reward_scaled_entry * current_element
    )
    payload_derivative = (
        expansion_ratio * cotangent_seed[0] + reward_scaled_entry * dividend_adjoint_sum
    )
    summed_dimensions = (0, 2)
    reward_piecewise_exponent = jnp.sum(reward_scaled_entry * current_element, summed_dimensions)
    fading_segment_exponent = (
        -jnp.exp(-fading_multiplier)
        * fading_multiplier
        * jnp.sum(
            carried_snapshots[0] * cotangent_seed[0] + carried_snapshots[1] * cotangent_seed[1],
            summed_dimensions,
        )
    )
    return (
        address_derivative,
        payload_derivative,
        reward_piecewise_exponent,
        fading_segment_exponent,
    )


def scatter_grads(fresh):
    return (
        lax.psum_scatter(fresh[0], ("seq", "rep"), scatter_dimension=0, tiled=True),
        lax.psum_scatter(fresh[1], ("seq", "rep"), scatter_dimension=0, tiled=True),
        lax.psum_scatter(fresh[2], ("seq", "rep"), scatter_dimension=0, tiled=True),
        lax.psum_scatter(fresh[3], ("seq", "rep"), scatter_dimension=0, tiled=True),
        lax.psum_scatter(fresh[4], ("seq", "rep"), scatter_dimension=0, tiled=True),
        lax.psum_scatter(fresh[5], ("seq", "rep"), scatter_dimension=0, tiled=True),
        lax.psum_scatter(fresh[6], ("seq", "rep"), scatter_dimension=0, tiled=True),
        lax.psum_scatter(fresh[7], ("seq", "rep"), scatter_dimension=0, tiled=True),
        lax.psum_scatter(fresh[8], ("seq", "rep"), scatter_dimension=0, tiled=True),
        lax.psum_scatter(fresh[9], ("seq", "rep"), scatter_dimension=0, tiled=True),
        lax.psum_scatter(fresh[10], ("seq", "rep"), scatter_dimension=0, tiled=True),
        lax.psum_scatter(fresh[11], ("seq", "rep"), scatter_dimension=0, tiled=True),
        lax.psum_scatter(fresh[12], ("seq", "rep"), scatter_dimension=0, tiled=True),
        lax.psum_scatter(fresh[13], ("seq", "rep"), scatter_dimension=0, tiled=True),
        lax.psum_scatter(fresh[14], ("seq", "rep"), scatter_dimension=0, tiled=True),
        lax.psum_scatter(fresh[15], ("seq", "rep"), scatter_dimension=0, tiled=True),
        lax.psum_scatter(fresh[16], ("seq", "rep"), scatter_dimension=0, tiled=True),
        lax.psum_scatter(fresh[17], ("seq", "rep"), scatter_dimension=0, tiled=True),
    )


def body(
    tokens,
    mixer_gain,
    mixer_bias,
    key_blend,
    value_blend,
    gate_blend,
    time_decay,
    time_first,
    key_weight,
    value_weight,
    gate_weight,
    output_weight,
    channel_gain,
    channel_bias,
    hidden_blend,
    screen_blend,
    hidden_weight,
    screen_weight,
    return_weight,
    cotangent,
):
    shard_list = (
        mixer_gain,
        mixer_bias,
        key_blend,
        value_blend,
        gate_blend,
        time_decay,
        time_first,
        key_weight,
        value_weight,
        gate_weight,
        output_weight,
        channel_gain,
        channel_bias,
        hidden_blend,
        screen_blend,
        hidden_weight,
        screen_weight,
        return_weight,
    )
    gathered = (
        lax.all_gather(mixer_gain, ("seq", "rep"), axis=0, tiled=True),
        lax.all_gather(mixer_bias, ("seq", "rep"), axis=0, tiled=True),
        lax.all_gather(key_blend, ("seq", "rep"), axis=0, tiled=True),
        lax.all_gather(value_blend, ("seq", "rep"), axis=0, tiled=True),
        lax.all_gather(gate_blend, ("seq", "rep"), axis=0, tiled=True),
        lax.all_gather(time_decay, ("seq", "rep"), axis=0, tiled=True),
        lax.all_gather(time_first, ("seq", "rep"), axis=0, tiled=True),
        lax.all_gather(key_weight, ("seq", "rep"), axis=0, tiled=True),
        lax.all_gather(value_weight, ("seq", "rep"), axis=0, tiled=True),
        lax.all_gather(gate_weight, ("seq", "rep"), axis=0, tiled=True),
        lax.all_gather(output_weight, ("seq", "rep"), axis=0, tiled=True),
        lax.all_gather(channel_gain, ("seq", "rep"), axis=0, tiled=True),
        lax.all_gather(channel_bias, ("seq", "rep"), axis=0, tiled=True),
        lax.all_gather(hidden_blend, ("seq", "rep"), axis=0, tiled=True),
        lax.all_gather(screen_blend, ("seq", "rep"), axis=0, tiled=True),
        lax.all_gather(hidden_weight, ("seq", "rep"), axis=0, tiled=True),
        lax.all_gather(screen_weight, ("seq", "rep"), axis=0, tiled=True),
        lax.all_gather(return_weight, ("seq", "rep"), axis=0, tiled=True),
    )
    vectors = [
        gathered[position].astype(jnp.float32) for position in (0, 1, 2, 3, 4, 5, 6, 11, 12, 13, 14)
    ]
    (
        mixer_g,
        mixer_b,
        key_share,
        value_share,
        gate_share,
        decay_log,
        temporal_reward_exponent,
        channel_g,
        channel_b,
        hidden_share,
        screen_share,
    ) = vectors
    full_key, full_value, full_gate, full_output = (
        gathered[7],
        gathered[8],
        gathered[9],
        gathered[10],
    )
    full_hidden, full_screen, full_return = (gathered[15], gathered[16], gathered[17])
    fading_multiplier = jnp.exp(decay_log)
    group_count, stretch_count, span_rows, model_width = tokens.shape
    lane_count = lax.axis_size("seq")
    lane_index = lax.axis_index("seq")
    is_first = lane_index == 0
    is_last = lane_index == lane_count - 1
    stretch_len = span_rows * lane_count
    segment_length = model_width // lane_count
    opening_offset = lane_index * segment_length
    rate_share = lax.dynamic_slice_in_dim(fading_multiplier, opening_offset, segment_length)
    reward_segment_exponent = lax.dynamic_slice_in_dim(
        temporal_reward_exponent, opening_offset, segment_length
    )
    spread_block = math.gcd(stretch_len, 128)
    stretch_positions = jnp.arange(stretch_len, dtype=jnp.float32)
    share_factor = jnp.exp(-stretch_len * rate_share)
    pending_one = jnp.zeros((group_count, model_width), jnp.float32)
    pending_two = jnp.zeros((group_count, model_width), jnp.float32)
    state_slice = jnp.zeros((2, group_count, segment_length), jnp.float32)
    share_top = jnp.zeros((group_count, segment_length), jnp.float32)
    stored = []
    outputs = []
    for micro_step in range(stretch_count):
        inputs = tokens[:, micro_step].astype(jnp.float32)
        normed_one, scaled_one, inverse_one = norm_rows(inputs, mixer_g, mixer_b)
        arrived_one = from_behind(normed_one[:, -1, :], "seq", 1)
        entering_one = jnp.where(is_first, pending_one, arrived_one)
        pending_one = arrived_one
        before_one = jnp.concatenate([entering_one[:, None, :], normed_one[:, :-1, :]], 1)
        key_input = blend(normed_one, before_one, key_share).astype(jnp.bfloat16)
        value_input = blend(normed_one, before_one, value_share).astype(jnp.bfloat16)
        gate_input = blend(normed_one, before_one, gate_share).astype(jnp.bfloat16)
        address_matrix_tile = product(key_input, full_key).astype(jnp.bfloat16)
        payload_matrix_tile = product(value_input, full_value).astype(jnp.bfloat16)
        gate_logit = product(gate_input, full_gate)
        arrived_rows = (
            lax.all_to_all(
                jnp.swapaxes(address_matrix_tile, 1, 2),
                "seq",
                split_axis=1,
                concat_axis=2,
                tiled=True,
            ),
            lax.all_to_all(
                jnp.swapaxes(payload_matrix_tile, 1, 2),
                "seq",
                split_axis=1,
                concat_axis=2,
                tiled=True,
            ),
        )
        key_portion_term = arrived_rows[0].astype(jnp.float32)
        value_portion_term = arrived_rows[1].astype(jnp.float32)
        precomputed_exponentials, inner_quantity, cumulative_sums, aggregate_result = wkv_prepare(
            key_portion_term, value_portion_term, rate_share, spread_block
        )
        raw_part, carried_snapshots = weighted_value_complete(
            key_portion_term,
            value_portion_term,
            reward_segment_exponent,
            precomputed_exponentials,
            inner_quantity,
            cumulative_sums,
            state_slice,
        )
        state_slice = share_factor * state_slice + aggregate_result
        local_top = jnp.max(
            key_portion_term
            - (stretch_len - 1.0 - stretch_positions)[None, :] * rate_share[:, None],
            2,
        )
        if micro_step == 0:
            share_top = local_top
        else:
            share_top = jnp.maximum(share_top - stretch_len * rate_share, local_top)
        wkv_kept = (
            precomputed_exponentials,
            carried_snapshots,
            key_portion_term,
            value_portion_term,
        )
        returned_rows = lax.all_to_all(
            raw_part.astype(jnp.bfloat16), "seq", split_axis=2, concat_axis=1, tiled=True
        )
        blended_input = jnp.swapaxes(returned_rows, 1, 2)
        mixture_wide = blended_input.astype(jnp.float32)
        gate_value = jax.nn.sigmoid(gate_logit)
        gated = (gate_value * mixture_wide).astype(jnp.bfloat16)
        residual = inputs + product(gated, full_output)
        normed_two, scaled_two, inverse_two = norm_rows(residual, channel_g, channel_b)
        arrived_two = from_behind(normed_two[:, -1, :], "seq", 1)
        entering_two = jnp.where(is_first, pending_two, arrived_two)
        pending_two = arrived_two
        before_two = jnp.concatenate([entering_two[:, None, :], normed_two[:, :-1, :]], 1)
        hidden_input = blend(normed_two, before_two, hidden_share).astype(jnp.bfloat16)
        screen_input = blend(normed_two, before_two, screen_share).astype(jnp.bfloat16)
        hidden_logit = product(hidden_input, full_hidden)
        hidden_act = jnp.square(jnp.maximum(hidden_logit, 0.0)).astype(jnp.bfloat16)
        returned = product(hidden_act, full_return)
        screen_value = jax.nn.sigmoid(product(screen_input, full_screen))
        outputs.append((residual + screen_value * returned).astype(jnp.bfloat16))
        stored.append(
            (
                normed_one - before_one,
                scaled_one,
                inverse_one,
                key_input,
                value_input,
                gate_input,
                gate_value,
                mixture_wide,
                gated,
                normed_two - before_two,
                scaled_two,
                inverse_two,
                hidden_input,
                screen_input,
                hidden_logit,
                hidden_act,
                returned,
                screen_value,
                wkv_kept,
            )
        )
    total_grads = tuple((jnp.zeros(piece.shape, jnp.float32) for piece in gathered))
    owned_grads = tuple((jnp.zeros(piece.shape, jnp.float32) for piece in shard_list))
    pending_back_one = jnp.zeros((group_count, model_width), jnp.float32)
    pending_back_two = jnp.zeros((group_count, model_width), jnp.float32)
    share_adjoint = jnp.zeros((2, group_count, segment_length), jnp.float32)
    input_grads = [None] * stretch_count
    for micro_step in range(stretch_count - 1, -1, -1):
        (
            spread_one,
            scaled_one,
            inverse_one,
            key_input,
            value_input,
            gate_input,
            gate_value,
            mixture_wide,
            gated,
            spread_two,
            scaled_two,
            inverse_two,
            hidden_input,
            screen_input,
            hidden_logit,
            hidden_act,
            returned,
            screen_value,
            wkv_kept,
        ) = stored[micro_step]
        upstream = cotangent[:, micro_step].astype(jnp.float32)
        returned_grad = (upstream * screen_value).astype(jnp.bfloat16)
        screen_grad = (upstream * returned * screen_value * (1.0 - screen_value)).astype(
            jnp.bfloat16
        )
        return_weight_grad = weight_grad(hidden_act, returned_grad)
        hidden_grad = (
            product_back(returned_grad, full_return) * 2.0 * jnp.maximum(hidden_logit, 0.0)
        ).astype(jnp.bfloat16)
        hidden_weight_grad = weight_grad(hidden_input, hidden_grad)
        screen_weight_grad = weight_grad(screen_input, screen_grad)
        hidden_back = product_back(hidden_grad, full_hidden)
        screen_back = product_back(screen_grad, full_screen)
        hidden_blend_grad = jnp.sum(hidden_back * spread_two, (0, 1))
        screen_blend_grad = jnp.sum(screen_back * spread_two, (0, 1))
        before_grad_two = hidden_back * (1.0 - hidden_share) + screen_back * (1.0 - screen_share)
        arrived_back_two = from_behind(before_grad_two[:, 0, :], "seq", -1)
        leaving_two = jnp.where(is_last, pending_back_two, arrived_back_two)
        pending_back_two = arrived_back_two
        normed_grad_two = (
            hidden_back * hidden_share
            + screen_back * screen_share
            + jnp.concatenate([before_grad_two[:, 1:, :], leaving_two[:, None, :]], 1)
        )
        channel_gain_grad = jnp.sum(normed_grad_two * scaled_two, (0, 1))
        channel_bias_grad = jnp.sum(normed_grad_two, (0, 1))
        residual_grad = upstream + norm_back(normed_grad_two, scaled_two, inverse_two, channel_g)
        output_grad = residual_grad.astype(jnp.bfloat16)
        output_weight_grad = weight_grad(gated, output_grad)
        gated_grad = product_back(output_grad, full_output)
        mixture_grad = (gated_grad * gate_value).astype(jnp.bfloat16)
        gate_grad = (gated_grad * mixture_wide * gate_value * (1.0 - gate_value)).astype(
            jnp.bfloat16
        )
        precomputed_exponentials, carried_snapshots, key_portion_term, value_portion_term = wkv_kept
        landed_gradient = lax.all_to_all(
            jnp.swapaxes(mixture_grad, 1, 2), "seq", split_axis=1, concat_axis=2, tiled=True
        )
        (
            dividend_adjoint_sum,
            divisor_adjoint_sum,
            reward_scaled_entry,
            reverse_inner_sums,
            reverse_accumulators,
            reverse_aggregate,
        ) = weighted_value_gradient_setup(
            landed_gradient.astype(jnp.float32),
            key_portion_term,
            value_portion_term,
            reward_segment_exponent,
            carried_snapshots,
            precomputed_exponentials,
        )
        (
            address_segment_derivative,
            payload_segment_derivative,
            reward_piecewise_exponent,
            fading_segment_exponent,
        ) = weighted_value_gradient_complete(
            key_portion_term,
            value_portion_term,
            rate_share,
            dividend_adjoint_sum,
            divisor_adjoint_sum,
            reward_scaled_entry,
            carried_snapshots,
            precomputed_exponentials,
            reverse_inner_sums,
            reverse_accumulators,
            share_adjoint,
        )
        share_adjoint = share_factor * share_adjoint + reverse_aggregate
        back_rows = (
            lax.all_to_all(
                address_segment_derivative.astype(jnp.bfloat16),
                "seq",
                split_axis=2,
                concat_axis=1,
                tiled=True,
            ),
            lax.all_to_all(
                payload_segment_derivative.astype(jnp.bfloat16),
                "seq",
                split_axis=2,
                concat_axis=1,
                tiled=True,
            ),
        )
        address_derivative = jnp.swapaxes(back_rows[0], 1, 2)
        payload_derivative = jnp.swapaxes(back_rows[1], 1, 2)
        null_array = jnp.zeros_like(temporal_reward_exponent)
        time_first_gradient = lax.dynamic_update_slice_in_dim(
            null_array, reward_piecewise_exponent, opening_offset, 0
        )
        time_decay_grad = lax.dynamic_update_slice_in_dim(
            null_array, fading_segment_exponent, opening_offset, 0
        )
        key_weight_grad = weight_grad(key_input, address_derivative)
        value_weight_grad = weight_grad(value_input, payload_derivative)
        gate_weight_grad = weight_grad(gate_input, gate_grad)
        key_back = product_back(address_derivative, full_key)
        value_back = product_back(payload_derivative, full_value)
        gate_back = product_back(gate_grad, full_gate)
        key_blend_grad = jnp.sum(key_back * spread_one, (0, 1))
        value_blend_grad = jnp.sum(value_back * spread_one, (0, 1))
        gate_blend_grad = jnp.sum(gate_back * spread_one, (0, 1))
        before_grad_one = (
            key_back * (1.0 - key_share)
            + value_back * (1.0 - value_share)
            + gate_back * (1.0 - gate_share)
        )
        arrived_back_one = from_behind(before_grad_one[:, 0, :], "seq", -1)
        leaving_one = jnp.where(is_last, pending_back_one, arrived_back_one)
        pending_back_one = arrived_back_one
        normed_grad_one = (
            key_back * key_share
            + value_back * value_share
            + gate_back * gate_share
            + jnp.concatenate([before_grad_one[:, 1:, :], leaving_one[:, None, :]], 1)
        )
        mixer_gain_grad = jnp.sum(normed_grad_one * scaled_one, (0, 1))
        mixer_bias_grad = jnp.sum(normed_grad_one, (0, 1))
        input_grads[micro_step] = residual_grad + norm_back(
            normed_grad_one, scaled_one, inverse_one, mixer_g
        )
        fresh = (
            mixer_gain_grad,
            mixer_bias_grad,
            key_blend_grad,
            value_blend_grad,
            gate_blend_grad,
            time_decay_grad,
            time_first_gradient,
            key_weight_grad,
            value_weight_grad,
            gate_weight_grad,
            output_weight_grad,
            channel_gain_grad,
            channel_bias_grad,
            hidden_blend_grad,
            screen_blend_grad,
            hidden_weight_grad,
            screen_weight_grad,
            return_weight_grad,
        )
        total_grads = tuple((running + portion for running, portion in zip(total_grads, fresh)))
    owned_grads = scatter_grads(total_grads)
    scaling = jnp.exp(-share_top)
    final_numerator = state_slice[0] * scaling
    final_denominator = state_slice[1] * scaling
    output = jnp.stack(outputs, 1)
    input_grad = jnp.stack(input_grads, 1)
    return (output, input_grad, final_numerator, final_denominator, share_top) + tuple(owned_grads)


def solution(mesh):
    in_specs = (
        P("rep", None, "seq", None),
        P(("seq", "rep")),
        P(("seq", "rep")),
        P(("seq", "rep")),
        P(("seq", "rep")),
        P(("seq", "rep")),
        P(("seq", "rep")),
        P(("seq", "rep")),
        P(("seq", "rep"), None),
        P(("seq", "rep"), None),
        P(("seq", "rep"), None),
        P(("seq", "rep"), None),
        P(("seq", "rep")),
        P(("seq", "rep")),
        P(("seq", "rep")),
        P(("seq", "rep")),
        P(("seq", "rep"), None),
        P(("seq", "rep"), None),
        P(("seq", "rep"), None),
        P("rep", None, "seq", None),
    )
    out_specs = (
        P("rep", None, "seq", None),
        P("rep", None, "seq", None),
        P("rep", "seq"),
        P("rep", "seq"),
        P("rep", "seq"),
        P(("seq", "rep")),
        P(("seq", "rep")),
        P(("seq", "rep")),
        P(("seq", "rep")),
        P(("seq", "rep")),
        P(("seq", "rep")),
        P(("seq", "rep")),
        P(("seq", "rep"), None),
        P(("seq", "rep"), None),
        P(("seq", "rep"), None),
        P(("seq", "rep"), None),
        P(("seq", "rep")),
        P(("seq", "rep")),
        P(("seq", "rep")),
        P(("seq", "rep")),
        P(("seq", "rep"), None),
        P(("seq", "rep"), None),
        P(("seq", "rep"), None),
    )
    return jax.shard_map(body, mesh=mesh, in_specs=in_specs, out_specs=out_specs, check_vma=False)
```

profile of v0, /device:TPU:0, one launch (start us, length us, event | category | flops | bytes accessed | tf_op | source)
XLA Modules:
  0.0 1659.0 jit_solution(6244097963569032315)
XLA Ops:
  16.4 42.6 %all-reduce.23 = (bf16[768]{0:T(1024)(128)(2,1)S(1)}, bf16[768]{0:T(1024)(128)(2,1)S(1)}, bf16[768]{0:T(1024)(128)(2,1)S(1)}, bf16[768]{0:T(1024)(128)(2,1)S(1)}...) all-reduce(bf16[768]{0:T(1024)(128)(2,1)S(1)} %dynamic-update-slice, ...), channel_id=1, replica_groups=mesh['seq'=16,'rep'=2] {'seq','rep'}, use_global_device_ids=true, to_apply=%add.6 | all-reduce | flops 8448 | bytes 33792
  75.1 4.8 add_convert_fusion.5
  88.9 38.9 %all-gather.10.cloned.1.call-done = bf16[768,768]{1,0:T(8,128)(2,1)} async-done(((bf16[24,768]{1,0:T(8,128)(2,1)}), bf16[768,768]{1,0:T(8,128)(2,1)}) %all-gather.10.cloned.1.call-update) | async-done | bytes 1179664 | tf_op jit(solution)/shard_map/all_gather | solution.py:296
  134.6 4.7 all-to-all-start
  146.7 13.1 all-to-all-done
  159.8 5.8 all-to-all-start.4
  177.0 10.5 all-to-all-done.4
  187.4 5.5 all-to-all-start.3
  203.6 4.6 copy.581
  208.2 5.6 copy.578
  220.3 4.6 reshape.1001
  224.9 5.6 copy.574
  230.6 5.8 copy.580
  247.4 5.8 copy.607
  253.3 5.6 copy.611
  265.4 4.6 reshape.1005
  269.9 5.6 copy.603
  275.5 5.6 copy.610
  290.4 41.8 %fusion.31 = f32[48,1,2,8,8]{4,1,3,2,0:T(1,128)S(1)} fusion(f32[128,48,1,1,1]{0,2,4,3,1:T(1,128)S(1)} %copy-done.128, f32[1,8,48,8,128]{4,3,1,0,2:T(8,128)S(1)} %get-tuple-element.253, f32[1,8,48,8,128]{4,3,1,0,2:T(8,128)S(1)} %get-tuple-element.252), kind=kOutput, calls=%fused_computation.51 | convolution fusion | flops 10223616 | bytes 3194880 | tf_op jit(solution)/shard_map/ic,...cmi->...cm/dot_general | solution.py:112
  332.8 6.9 bitcast_add_fusion.5
  355.6 41.6 %fusion.30 = f32[48,1,2,8,8]{4,1,3,2,0:T(1,128)S(1)} fusion(f32[128,48,1,1,1]{0,2,4,3,1:T(1,128)S(1)} %copy-done.129, f32[1,8,48,8,128]{4,3,1,0,2:T(8,128)S(1)} %get-tuple-element.255, f32[1,8,48,8,128]{4,3,1,0,2:T(8,128)S(1)} %get-tuple-element.254), kind=kOutput, calls=%fused_computation.50 | convolution fusion | flops 10223616 | bytes 3194880 | tf_op jit(solution)/shard_map/ic,...cmi->...cm/dot_general | solution.py:112
  400.4 6.8 bitcast_add_fusion.4
  420.3 8.9 divide_convert_fusion.1
  435.6 7.0 all-to-all-start.2
  448.2 12.8 all-to-all-done.2
  490.2 4.6 reshape.1081
  499.4 5.5 copy.616
  527.4 7.9 fusion.10
  535.3 7.9 fusion.2
  554.0 7.3 fusion.6
  561.4 7.4 multiply_convert_fusion.3
  575.1 5.5 multiply_convert_fusion.1
  610.2 5.3 all-to-all-start.6
  618.2 4.6 fusion.137
  626.8 5.4 all-to-all-done.6
  651.1 5.6 copy.648
  663.3 4.6 reshape.1010
  667.8 5.6 copy.644
  673.4 5.6 copy.663
  684.4 6.9 multiply_divide_fusion.1
  691.3 41.6 %fusion.28 = f32[48,1,2,8,8]{4,1,3,2,0:T(1,128)S(1)} fusion(f32[128,48,1,1,1]{0,2,4,3,1:T(1,128)S(1)} %copy-done.130, f32[1,8,48,8,128]{4,3,1,0,2:T(8,128)S(1)} %get-tuple-element.298, f32[1,8,48,8,128]{4,3,1,0,2:T(8,128)S(1)} %get-tuple-element.299), kind=kOutput, calls=%fused_computation.48 | convolution fusion | flops 10223616 | bytes 3194880 | tf_op jit(solution)/shard_map/tc,...cmt->...cm/dot_general | solution.py:162
  736.1 43.7 %fusion.29 = f32[48,1,2,8,8]{4,1,3,2,0:T(1,128)S(1)} fusion(f32[128,48,1,1,1]{0,2,4,3,1:T(1,128)} %copy.735, f32[1,8,48,8,128]{4,3,1,0,2:T(8,128)} %get-tuple-element.201, f32[1,8,48,8,128]{4,3,1,0,2:T(8,128)} %get-tuple-element.202), kind=kOutput, calls=%fused_computation.49 | convolution fusion | flops 10223616 | bytes 3194880 | tf_op jit(solution)/shard_map/tc,...cmt->...cm/dot_general | solution.py:162
  801.1 5.4 bitcast_add_fusion.2
  812.7 15.8 fusion.66
  835.0 7.0 all-to-all-start.10
  852.6 6.9 all-to-all-done.10
  859.5 4.8 all-to-all-start.11
  872.2 10.2 all-to-all-done.11
  897.7 10.2 all-to-all-done.8
  907.8 5.8 all-to-all-start.9
  913.7 8.8 fusion.26
  979.0 10.6 bitcast_add_fusion.1
  991.5 5.5 fusion.134
  997.0 5.3 bitcast_add_fusion
  1011.8 5.7 copy.691
  1021.5 5.7 copy.693
  1034.5 14.7 multiply_reduce_fusion.1
  1057.5 5.5 collective-permute-start.6
  1082.4 39.5 %all-reduce.22 = (f32[768]{0:T(1024)S(1)}, f32[768]{0:T(1024)S(1)}, f32[768]{0:T(1024)S(1)}, f32[768]{0:T(1024)S(1)}, f32[768]{0:T(1024)S(1)}, /*index=5*/f32[76...) all-reduce(f32[768]{0:T(1024)S(1)} %add.594, ...), channel_id=2, replica_groups=mesh['seq'=16,'rep'=2] {'seq','rep'}, use_global_device_ids=true, to_apply=%region_20.21.clone | all-reduce | flops 8448 | bytes 67584
  1128.3 32.5 %reduce-scatter.14.cloned.1.call-done = f32[24,768]{1,0:T(8,128)} async-done(((f32[768,768]{1,0:T(8,128)}), f32[24,768]{1,0:T(8,128)}) %reduce-scatter.14.cloned.1.call-update) | async-done | bytes 73744 | tf_op jit(solution)/shard_map/reduce_scatter | solution.py:235
  1160.8 104.8 %reduce-scatter.8.cloned.1.call-done = f32[24,768]{1,0:T(8,128)} async-done(((f32[768,768]{1,0:T(8,128)}), f32[24,768]{1,0:T(8,128)}) %reduce-scatter.8.cloned.1.call-update) | async-done | bytes 73744 | tf_op jit(solution)/shard_map/reduce_scatter | solution.py:232
  1265.5 103.7 %reduce-scatter.10.cloned.1.call-done = f32[24,768]{1,0:T(8,128)} async-done(((f32[768,768]{1,0:T(8,128)}), f32[24,768]{1,0:T(8,128)}) %reduce-scatter.10.cloned.1.call-update) | async-done | bytes 73744 | tf_op jit(solution)/shard_map/reduce_scatter | solution.py:233
  1369.2 142.1 %reduce-scatter.16.cloned.1.call-done = f32[24,3072]{1,0:T(8,128)} async-done(((f32[768,3072]{1,0:T(8,128)}), f32[24,3072]{1,0:T(8,128)}) %reduce-scatter.16.cloned.1.call-update) | async-done | bytes 294928 | tf_op jit(solution)/shard_map/reduce_scatter | solution.py:240
  1511.3 141.0 %reduce-scatter.20.cloned.1.call-done = f32[96,768]{1,0:T(8,128)} async-done(((f32[3072,768]{1,0:T(8,128)}), f32[96,768]{1,0:T(8,128)}) %reduce-scatter.20.cloned.1.call-update) | async-done | bytes 294928 | tf_op jit(solution)/shard_map/reduce_scatter | solution.py:242
  (803 shorter events, 470.1 us)
Async XLA Ops:
  7.2 72.7 %all-gather.12.cloned.1.call-start = ((), (), s32[]{:S(2)}) async-start(), calls=%async_computation.21 | async-start | bytes 1216512 | tf_op jit(solution)/shard_map/all_gather | solution.py:297
  7.9 119.8 %all-gather.10.cloned.1.call-start = ((), (), s32[]{:S(2)}) async-start(), calls=%async_computation.20 | async-start | bytes 1216512 | tf_op jit(solution)/shard_map/all_gather | solution.py:296
  8.7 474.1 %all-gather.8.cloned.1.call-start = ((), (), s32[]{:S(2)}) async-start(), calls=%async_computation.19 | async-start | bytes 1216512 | tf_op jit(solution)/shard_map/all_gather | solution.py:298
  9.4 477.6 %all-gather.14.cloned.1.call-start = ((), (), s32[]{:S(2)}) async-start(), calls=%async_computation.22 | async-start | bytes 1216512 | tf_op jit(solution)/shard_map/all_gather | solution.py:299
  10.0 517.4 %all-gather.18.cloned.1.call-start = ((), (), s32[]{:S(2)}) async-start(), calls=%async_computation.24 | async-start | bytes 4866048 | tf_op jit(solution)/shard_map/all_gather | solution.py:304
  13.8 47.7 %copy-start.7 = (f32[8,64,768]{2,0,1:T(8,128)}, f32[8,64,768]{2,0,1:T(8,128)S(1)}, u32[]{:S(2)}) copy-start(f32[8,64,768]{2,0,1:T(8,128)S(1)} %get-tuple-element.259) | copy-start | bytes 4718596
  13.8 47.6 %copy-start.138 = (f32[8,64]{1,0:T(8,128)}, f32[8,64]{1,0:T(8,128)S(1)}, u32[]{:S(2)}) copy-start(f32[8,64]{1,0:T(8,128)S(1)} %copy.566) | copy-start | bytes 6148
  64.5 7.5 collective-permute-start
  66.8 7.6 collective-permute-start.2
  83.3 44.4 %copy-start.106 = (bf16[8,64,768]{2,0,1:T(8,128)(2,1)S(1)}, bf16[8,64,768]{2,0,1:T(8,128)(2,1)}, u32[]{:S(2)}) copy-start(bf16[8,64,768]{2,0,1:T(8,128)(2,1)} %get-tuple-element.271) | copy-start | bytes 2359300
  85.2 49.4 %all-to-all-start.1 = ((bf16[16,2,12288]{2,1,0:T(2,128)(2,1)}), bf16[16,2,12288]{2,1,0:T(2,128)(2,1)S(1)}, u32[]{:S(2)}, u32[]{:S(2)}) async-start(bf16[16,2,12288]{2,1,0:T(2,128)(2,1)} %reshape.1074), calls=%async_computation.1 | async-start | bytes 1572864 | tf_op jit(solution)/shard_map/all_to_all | solution.py:374
  134.6 25.2 %all-to-all-start = ((bf16[16,2,12288]{2,1,0:T(2,128)(2,1)}), bf16[16,2,12288]{2,1,0:T(2,128)(2,1)S(1)}, u32[]{:S(2)}, u32[]{:S(2)}) async-start(bf16[16,2,12288]{2,1,0:T(2,128)(2,1)} %reshape.1072), calls=%async_computation | async-start | bytes 1572864 | tf_op jit(solution)/shard_map/all_to_all | solution.py:367
  139.3 396.0 %all-gather.20.cloned.1.call-start = ((), (), s32[]{:S(2)}) async-start(), calls=%async_computation.25 | async-start | bytes 4866048 | tf_op jit(solution)/shard_map/all_gather | solution.py:306
  146.7 23.4 %copy-start.108 = (bf16[8,64,768]{2,0,1:T(8,128)(2,1)S(1)}, bf16[8,64,768]{2,0,1:T(8,128)(2,1)}, u32[]{:S(2)}) copy-start(bf16[8,64,768]{2,0,1:T(8,128)(2,1)} %get-tuple-element.247) | copy-start | bytes 2359300
  159.8 27.6 %all-to-all-start.4 = ((bf16[16,2,12288]{2,1,0:T(2,128)(2,1)}), bf16[16,2,12288]{2,1,0:T(2,128)(2,1)}, u32[]{:S(2)}, u32[]{:S(2)}) async-start(bf16[16,2,12288]{2,1,0:T(2,128)(2,1)} %reshape.1078), calls=%async_computation.4 | async-start | bytes 1572864 | tf_op jit(solution)/shard_map/all_to_all | solution.py:374
  166.2 232.9 %copy-start.157 = (f32[48]{0:T(128)}, f32[48]{0:T(128)S(1)}, u32[]{:S(2)}) copy-start(f32[48]{0:T(128)S(1)} %get-tuple-element.197) | copy-start | bytes 580
  168.2 230.4 %copy-start.180 = (f32[48]{0:T(128)}, f32[48]{0:T(128)S(1)}, u32[]{:S(2)}) copy-start(f32[48]{0:T(128)S(1)} %get-tuple-element.308) | copy-start | bytes 580
  187.4 71.4 %all-to-all-start.3 = ((bf16[16,2,12288]{2,1,0:T(2,128)(2,1)}), bf16[16,2,12288]{2,1,0:T(2,128)(2,1)}, u32[]{:S(2)}, u32[]{:S(2)}) async-start(bf16[16,2,12288]{2,1,0:T(2,128)(2,1)} %reshape.1076), calls=%async_computation.3 | async-start | bytes 1572864 | tf_op jit(solution)/shard_map/all_to_all | solution.py:367
  195.7 202.8 %copy-start.154 = (f32[8,8]{1,0:T(8,128)}, f32[8,8]{1,0:T(8,128)S(1)}, u32[]{:S(2)}) copy-start(f32[8,8]{1,0:T(8,128)S(1)} %maximum_negate_fusion.1) | copy-start | bytes 772
  290.4 41.8 %copy-start.135 = (f32[48,8]{1,0:T(8,128)S(1)}, f32[48,8]{1,0:T(8,128)}, u32[]{:S(2)}) copy-start(f32[48,8]{1,0:T(8,128)} %copy.579) | copy-start | bytes 4612
  290.4 41.8 %copy-start.193 = (pred[8,8]{1,0:T(8,128)(4,1)S(1)}, pred[8,8]{1,0:T(8,128)(4,1)}, u32[]{:S(2)}) copy-start(pred[8,8]{1,0:T(8,128)(4,1)} %fusion.197) | copy-start | bytes 196
  290.4 42.4 %copy-start.150 = (f32[128,128]{1,0:T(8,128)S(1)}, f32[128,128]{1,0:T(8,128)}, u32[]{:S(2)}) copy-start(f32[128,128]{1,0:T(8,128)} %maximum_negate_fusion) | copy-start | bytes 196612
  290.4 42.4 %copy-start.162 = (f32[48,128]{1,0:T(8,128)S(1)}, f32[48,128]{1,0:T(8,128)}, u32[]{:S(2)}) copy-start(f32[48,128]{1,0:T(8,128)} %get-tuple-element.301) | copy-start | bytes 73732
  290.4 42.4 %copy-start.174 = (pred[128,128]{1,0:T(8,128)(4,1)S(1)}, pred[128,128]{1,0:T(8,128)(4,1)}, u32[]{:S(2)}) copy-start(pred[128,128]{1,0:T(8,128)(4,1)} %fusion.194) | copy-start | bytes 49156
  355.6 41.7 %copy-start.54 = (f32[1,8,48,8,128]{4,3,1,0,2:T(8,128)}, f32[1,8,48,8,128]{4,3,1,0,2:T(8,128)S(1)}, u32[]{:S(2)}) copy-start(f32[1,8,48,8,128]{4,3,1,0,2:T(8,128)S(1)} %get-tuple-element.254) | copy-start | bytes 4718596
  355.6 41.7 %copy-start.56 = (f32[1,8,48,8,128]{4,3,1,0,2:T(8,128)}, f32[1,8,48,8,128]{4,3,1,0,2:T(8,128)S(1)}, u32[]{:S(2)}) copy-start(f32[1,8,48,8,128]{4,3,1,0,2:T(8,128)S(1)} %get-tuple-element.255) | copy-start | bytes 4718596
  355.6 41.7 %copy-start.137 = (f32[48,8]{1,0:T(8,128)S(1)}, f32[48,8]{1,0:T(8,128)}, u32[]{:S(2)}) copy-start(f32[48,8]{1,0:T(8,128)} %copy.760) | copy-start | bytes 4612
  355.6 42.2 %copy-start.192 = (f32[48]{0:T(128)S(1)}, f32[48]{0:T(128)}, u32[]{:S(2)}) copy-start(f32[48]{0:T(128)} %get-tuple-element.306) | copy-start | bytes 580
  355.6 42.2 %copy-start.198 = (f32[48]{0:T(128)S(1)}, f32[48]{0:T(128)}, u32[]{:S(2)}) copy-start(f32[48]{0:T(128)} %get-tuple-element.307) | copy-start | bytes 580
  355.6 42.9 %copy-start.161 = (f32[48,8]{1,0:T(8,128)S(1)}, f32[48,8]{1,0:T(8,128)}, u32[]{:S(2)}) copy-start(f32[48,8]{1,0:T(8,128)} %copy.608) | copy-start | bytes 4612
  355.6 42.9 %copy-start.194 = (pred[8,8]{1,0:T(8,128)(4,1)S(1)}, pred[8,8]{1,0:T(8,128)(4,1)}, u32[]{:S(2)}) copy-start(pred[8,8]{1,0:T(8,128)(4,1)} %fusion.197) | copy-start | bytes 196
  435.6 25.4 %all-to-all-start.2 = ((bf16[16,2,12288]{2,1,0:T(2,128)(2,1)}), bf16[16,2,12288]{2,1,0:T(2,128)(2,1)}, u32[]{:S(2)}, u32[]{:S(2)}) async-start(bf16[16,2,12288]{2,1,0:T(2,128)(2,1)} %reshape.1082), calls=%async_computation.2 | async-start | bytes 1572864 | tf_op jit(solution)/shard_map/all_to_all | solution.py:412
  461.0 29.2 %all-to-all-start.5 = ((bf16[16,2,12288]{2,1,0:T(2,128)(2,1)}), bf16[16,2,12288]{2,1,0:T(2,128)(2,1)}, u32[]{:S(2)}, u32[]{:S(2)}) async-start(bf16[16,2,12288]{2,1,0:T(2,128)(2,1)} %reshape.1080), calls=%async_computation.5 | async-start | bytes 1572864 | tf_op jit(solution)/shard_map/all_to_all | solution.py:412
  465.4 77.8 %all-gather.16.cloned.1.call-start = ((), (), s32[]{:S(2)}) async-start(), calls=%async_computation.23 | async-start | bytes 1216512 | tf_op jit(solution)/shard_map/all_gather | solution.py:305
  515.6 7.5 collective-permute-start.1
  517.6 7.4 collective-permute-start.3
  550.6 34.0 %copy-start.68 = (f32[8,64,768]{2,0,1:T(8,128)}, f32[8,64,768]{2,0,1:T(8,128)S(1)}, u32[]{:S(2)}) copy-start(f32[8,64,768]{2,0,1:T(8,128)S(1)} %fusion.99) | copy-start | bytes 4718596
  587.6 5.0 collective-permute-start.4
  589.2 3.8 collective-permute-start.5
  610.2 22.0 %all-to-all-start.6 = ((bf16[16,2,12288]{2,1,0:T(2,128)(2,1)}), bf16[16,2,12288]{2,1,0:T(2,128)(2,1)}, u32[]{:S(2)}, u32[]{:S(2)}) async-start(bf16[16,2,12288]{2,1,0:T(2,128)(2,1)} %reshape.1084), calls=%async_computation.6 | async-start | bytes 1572864 | tf_op jit(solution)/shard_map/all_to_all | solution.py:518
  632.2 24.6 %all-to-all-start.7 = ((bf16[16,2,12288]{2,1,0:T(2,128)(2,1)}), bf16[16,2,12288]{2,1,0:T(2,128)(2,1)}, u32[]{:S(2)}, u32[]{:S(2)}) async-start(bf16[16,2,12288]{2,1,0:T(2,128)(2,1)} %reshape.1086), calls=%async_computation.7 | async-start | bytes 1572864 | tf_op jit(solution)/shard_map/all_to_all | solution.py:518
  691.3 41.7 %copy-start.48 = (f32[1,8,48,8,128]{4,3,1,0,2:T(8,128)}, f32[1,8,48,8,128]{4,3,1,0,2:T(8,128)S(1)}, u32[]{:S(2)}) copy-start(f32[1,8,48,8,128]{4,3,1,0,2:T(8,128)S(1)} %get-tuple-element.298) | copy-start | bytes 4718596
  691.3 41.6 %copy-start.50 = (f32[1,8,48,8,128]{4,3,1,0,2:T(8,128)}, f32[1,8,48,8,128]{4,3,1,0,2:T(8,128)S(1)}, u32[]{:S(2)}) copy-start(f32[1,8,48,8,128]{4,3,1,0,2:T(8,128)S(1)} %get-tuple-element.299) | copy-start | bytes 4718596
  691.3 41.7 %copy-start.136 = (f32[48,8]{1,0:T(8,128)S(1)}, f32[48,8]{1,0:T(8,128)}, u32[]{:S(2)}) copy-start(f32[48,8]{1,0:T(8,128)} %copy.761) | copy-start | bytes 4612
  736.0 43.8 %copy-start.153 = (f32[2,8,48]{1,0,2:T(2,128)S(1)}, f32[2,8,48]{1,0,2:T(2,128)}, u32[]{:S(2)}) copy-start(f32[2,8,48]{1,0,2:T(2,128)} %copy.645) | copy-start | bytes 9220
  736.0 43.8 %copy-start.155 = (f32[8,8]{1,0:T(8,128)S(1)}, f32[8,8]{1,0:T(8,128)}, u32[]{:S(2)}) copy-start(f32[8,8]{1,0:T(8,128)} %copy-done.154) | copy-start | bytes 772
  736.0 43.8 %copy-start.164 = (f32[48,8]{1,0:T(8,128)S(1)}, f32[48,8]{1,0:T(8,128)}, u32[]{:S(2)}) copy-start(f32[48,8]{1,0:T(8,128)} %copy.638) | copy-start | bytes 4612
  736.0 43.8 %copy-start.181 = (f32[48]{0:T(128)S(1)}, f32[48]{0:T(128)}, u32[]{:S(2)}) copy-start(f32[48]{0:T(128)} %copy-done.180) | copy-start | bytes 580
  736.1 43.8 %copy-start.195 = (pred[8,8]{1,0:T(8,128)(4,1)S(1)}, pred[8,8]{1,0:T(8,128)(4,1)}, u32[]{:S(2)}) copy-start(pred[8,8]{1,0:T(8,128)(4,1)} %fusion.197) | copy-start | bytes 196
  736.1 44.4 %copy-start.152 = (f32[128,128]{1,0:T(8,128)S(1)}, f32[128,128]{1,0:T(8,128)}, u32[]{:S(2)}) copy-start(f32[128,128]{1,0:T(8,128)} %maximum_negate_fusion) | copy-start | bytes 196612
  736.1 44.4 %copy-start.160 = (f32[48,128]{1,0:T(8,128)S(1)}, f32[48,128]{1,0:T(8,128)}, u32[]{:S(2)}) copy-start(f32[48,128]{1,0:T(8,128)} %get-tuple-element.300) | copy-start | bytes 73732
  835.0 24.5 %all-to-all-start.10 = ((bf16[16,2,12288]{2,1,0:T(2,128)(2,1)}), bf16[16,2,12288]{2,1,0:T(2,128)(2,1)}, u32[]{:S(2)}, u32[]{:S(2)}) async-start(bf16[16,2,12288]{2,1,0:T(2,128)(2,1)} %reshape.1090), calls=%async_computation.10 | async-start | bytes 1572864 | tf_op jit(solution)/shard_map/all_to_all | solution.py:556
  842.0 286.3 %reduce-scatter.18.cloned.1.call-start = ((), (), s32[]{:S(2)}) async-start(), calls=%async_computation.31 | async-start | bytes 2433024 | tf_op jit(solution)/shard_map/reduce_scatter | solution.py:241
  859.5 23.0 %all-to-all-start.11 = ((bf16[16,2,12288]{2,1,0:T(2,128)(2,1)}), bf16[16,2,12288]{2,1,0:T(2,128)(2,1)}, u32[]{:S(2)}, u32[]{:S(2)}) async-start(bf16[16,2,12288]{2,1,0:T(2,128)(2,1)} %reshape.1088), calls=%async_computation.11 | async-start | bytes 1572864 | tf_op jit(solution)/shard_map/all_to_all | solution.py:563
  882.5 25.4 %all-to-all-start.8 = ((bf16[16,2,12288]{2,1,0:T(2,128)(2,1)}), bf16[16,2,12288]{2,1,0:T(2,128)(2,1)}, u32[]{:S(2)}, u32[]{:S(2)}) async-start(bf16[16,2,12288]{2,1,0:T(2,128)(2,1)} %reshape.1094), calls=%async_computation.8 | async-start | bytes 1572864 | tf_op jit(solution)/shard_map/all_to_all | solution.py:556
  886.9 241.4 %reduce-scatter.12.cloned.1.call-start = ((), (), s32[]{:S(2)}) async-start(), calls=%async_computation.28 | async-start | bytes 2433024 | tf_op jit(solution)/shard_map/reduce_scatter | solution.py:234
  907.8 49.7 %all-to-all-start.9 = ((bf16[16,2,12288]{2,1,0:T(2,128)(2,1)}), bf16[16,2,12288]{2,1,0:T(2,128)(2,1)}, u32[]{:S(2)}, u32[]{:S(2)}) async-start(bf16[16,2,12288]{2,1,0:T(2,128)(2,1)} %reshape.1092), calls=%async_computation.9 | async-start | bytes 1572864 | tf_op jit(solution)/shard_map/all_to_all | solution.py:563
  913.6 247.1 %reduce-scatter.14.cloned.1.call-start = ((), (), s32[]{:S(2)}) async-start(), calls=%async_computation.29 | async-start | bytes 2433024 | tf_op jit(solution)/shard_map/reduce_scatter | solution.py:235
  926.1 339.4 %reduce-scatter.8.cloned.1.call-start = ((), (), s32[]{:S(2)}) async-start(), calls=%async_computation.26 | async-start | bytes 2433024 | tf_op jit(solution)/shard_map/reduce_scatter | solution.py:232
  972.9 396.3 %reduce-scatter.10.cloned.1.call-start = ((), (), s32[]{:S(2)}) async-start(), calls=%async_computation.27 | async-start | bytes 2433024 | tf_op jit(solution)/shard_map/reduce_scatter | solution.py:233
  977.9 533.4 %reduce-scatter.16.cloned.1.call-start = ((), (), s32[]{:S(2)}) async-start(), calls=%async_computation.30 | async-start | bytes 9732096 | tf_op jit(solution)/shard_map/reduce_scatter | solution.py:240
  989.6 662.6 %reduce-scatter.20.cloned.1.call-start = ((), (), s32[]{:S(2)}) async-start(), calls=%async_computation.32 | async-start | bytes 9732096 | tf_op jit(solution)/shard_map/reduce_scatter | solution.py:242
  1057.5 12.1 collective-permute-start.6
  1067.8 3.9 collective-permute-start.7
  (197 other events, 941.0 us)
Sparse Core Ops, SparseCore 0:
  10.9 56.9 all-gather.11
  70.8 56.9 all-gather.9
  130.6 57.0 all-gather.7
  190.5 54.6 all-gather.13
  247.9 62.5 all-gather.17
  313.3 62.4 all-gather.19
  469.1 55.3 all-gather.15
  848.7 103.3 reduce-scatter.17
  958.8 98.1 reduce-scatter.11
  1062.7 98.0 reduce-scatter.13
  1167.5 97.9 reduce-scatter.7
  1271.2 97.9 reduce-scatter.9
  1376.7 134.5 reduce-scatter.15
  1517.6 134.5 reduce-scatter.19
where the time goes:
time: 1670 us; the launch traced here: 1660 us
  waiting for transfers between devices  647 us (39%)
  local copies, waits for them, and re-layouts  389 us (23%)
  matrix products  349 us (21%)
  other arithmetic  95.5 us (6%)
  blocking collectives  82.1 us (5%)
  starting transfers between devices  79.5 us (5%)
  between operations  17.4 us (1%)
    reduce_scatter x1, waiting for transfers between devices, scatter_grads(): lax.psum_scatter(fresh[15], ('seq', 'rep'), scatter_dimension=0, tiled=True)  142 us
    reduce_scatter x1, waiting for transfers between devices, scatter_grads(): lax.psum_scatter(fresh[17], ('seq', 'rep'), scatter_dimension=0, tiled=True)  141 us
    unnamed x515, local copies, waits for them, and re-layouts  115 us
    reduce_scatter x1, waiting for transfers between devices, scatter_grads(): lax.psum_scatter(fresh[7], ('seq', 'rep'), scatter_dimension=0, tiled=True)  105 us
    reduce_scatter x1, waiting for transfers between devices, scatter_grads(): lax.psum_scatter(fresh[8], ('seq', 'rep'), scatter_dimension=0, tiled=True)  104 us
    dot_general x2, matrix products, weighted_value_gradient_setup(): cumulative_sums = jnp.einsum(texts[5], leading, blocked, precision=highest)  85.3 us
    dot_general x2, matrix products, wkv_prepare(): cumulative_sums = jnp.einsum(texts[1], trailing, blocked, precision=highest)  83.4 us
    unnamed x2, blocking collectives  82.1 us
  transfers between devices with their start and end apart: 34, of which 19 were waited for; matrix products, arithmetic and copies ran while one was open for 34% of the time, Pallas kernels for 0%

commit v1 on v0

v1 whole, which is shorter than its diff:
```python
import jax
import jax.numpy as jnp
from jax import lax
from jax.experimental import pallas as pl
from jax.experimental.pallas import tpu as pltpu
from jax.sharding import PartitionSpec as P

f32 = jnp.float32
bf16 = jnp.bfloat16
norm_eps = 1e-05
both = ("seq", "rep")


def mm(left, right):
    return jnp.dot(left, right, preferred_element_type=f32)


def mm_nt(left, right):
    return lax.dot_general(left, right, (((1,), (1,)), ((), ())), preferred_element_type=f32)


def mm_tn(left, right):
    return lax.dot_general(left, right, (((0,), (0,)), ((), ())), preferred_element_type=f32)


def normalise(values):
    centred = values - jnp.mean(values, -1, keepdims=True)
    inverse = lax.rsqrt(jnp.mean(centred * centred, -1, keepdims=True) + norm_eps)
    return centred * inverse, inverse


def norm_back(upstream, scaled, inverse, gain):
    inner = upstream * gain
    centred = inner - jnp.mean(inner, -1, keepdims=True)
    return inverse * (centred - scaled * jnp.mean(inner * scaled, -1, keepdims=True))


def ring(value, steps):
    count = lax.axis_size("seq")
    return lax.ppermute(value, "seq", [(i, (i + steps) % count) for i in range(count)])


def entering(last, spot):
    got = ring(last, 1)
    pairs = got.reshape(-1, 2, got.shape[-1])
    wrapped = jnp.concatenate([jnp.zeros_like(pairs[:, :1]), pairs[:, :1]], 1)
    return jnp.where(spot == 0, wrapped, pairs).reshape(got.shape)


def leaving(first, spot):
    count = lax.axis_size("seq")
    got = ring(first, -1)
    pairs = got.reshape(-1, 2, got.shape[-1])
    wrapped = jnp.concatenate([pairs[:, 1:], jnp.zeros_like(pairs[:, :1])], 1)
    return jnp.where(spot == count - 1, wrapped, pairs).reshape(got.shape)


def forward_kernel(k_ref, v_ref, carry_ref, decay_ref, first_ref, num_ref, den_ref, mix_ref):
    keep = jnp.exp(-jnp.exp(decay_ref[...]))
    boost_rate = jnp.exp(first_ref[...])

    def step(t, state):
        num, den = state
        k = jnp.exp(k_ref[t].astype(f32))
        v = v_ref[t].astype(f32)
        boost = k * boost_rate
        num_ref[t] = num
        den_ref[t] = den
        mix_ref[t] = (num + boost * v) / (den + boost)
        return keep * num + k * v, keep * den + k

    lax.fori_loop(0, k_ref.shape[0], step, (carry_ref[0], carry_ref[1]))


def backward_kernel(
    k_ref, v_ref, num_ref, den_ref, mix_ref, grad_ref, carry_ref, decay_ref, first_ref,
    kg_ref, vg_ref, first_grad_ref, decay_grad_ref,
):
    keep = jnp.exp(-jnp.exp(decay_ref[...]))
    boost_rate = jnp.exp(first_ref[...])
    length = k_ref.shape[0]

    def step(i, state):
        adj_num, adj_den, first_sum, decay_sum = state
        t = length - 1 - i
        k = jnp.exp(k_ref[t].astype(f32))
        v = v_ref[t].astype(f32)
        boost = k * boost_rate
        num_grad = grad_ref[t].astype(f32) / (den_ref[t] + boost)
        den_grad = -num_grad * mix_ref[t]
        inner = boost * (v * num_grad + den_grad)
        kg_ref[t] = (k * (v * adj_num + adj_den) + inner).astype(bf16)
        vg_ref[t] = (k * adj_num + boost * num_grad).astype(bf16)
        first_sum = first_sum + inner
        decay_sum = decay_sum + num_ref[t] * adj_num + den_ref[t] * adj_den
        return keep * adj_num + num_grad, keep * adj_den + den_grad, first_sum, decay_sum

    zero = jnp.zeros_like(carry_ref[0])
    out = lax.fori_loop(0, length, step, (carry_ref[0], carry_ref[1], zero, zero))
    first_grad_ref[...] = out[2]
    decay_grad_ref[...] = out[3]


def call(kernel, shapes, *operands):
    space = pl.BlockSpec(memory_space=pltpu.VMEM)
    return pl.pallas_call(
        kernel,
        out_shape=[jax.ShapeDtypeStruct(s, t) for s, t in shapes],
        in_specs=[space] * len(operands),
        out_specs=[space] * len(shapes),
        compiler_params=pltpu.CompilerParams(vmem_limit_bytes=48 * 2**20),
    )(*operands)


def body(
    tokens, mixer_gain, mixer_bias, key_blend, value_blend, gate_blend, time_decay, time_first,
    key_weight, value_weight, gate_weight, output_weight, channel_gain, channel_bias,
    hidden_blend, screen_blend, hidden_weight, screen_weight, return_weight, cotangent,
):
    groups, stretches, span, width = tokens.shape
    count = lax.axis_size("seq")
    owners = count * lax.axis_size("rep")
    spot = lax.axis_index("seq")
    segs = groups * stretches
    rows = span * segs
    own = width // owners
    inner = hidden_weight.shape[1]
    parts = inner // width

    vectors = (
        mixer_gain, mixer_bias, key_blend, value_blend, gate_blend, time_decay, time_first,
        channel_gain, channel_bias, hidden_blend, screen_blend,
    )
    squares = (key_weight, value_weight, gate_weight, output_weight, screen_weight)
    packed = jnp.concatenate(
        squares + (hidden_weight.reshape(own * parts, width), return_weight), 0
    )
    packed = lax.all_gather(packed, both, axis=0)
    spread_vectors = lax.all_gather(jnp.stack(vectors), both, axis=0)
    spread_vectors = jnp.swapaxes(spread_vectors, 0, 1).reshape(len(vectors), width).astype(f32)
    (
        mixer_g, mixer_b, key_share, value_share, gate_share, decay_log, first_log,
        channel_g, channel_b, hidden_share, screen_share,
    ) = [spread_vectors[i][None] for i in range(len(vectors))]

    def piece(start, size, shape):
        return packed[:, start : start + size].reshape(shape)

    w_key, w_value, w_gate, w_output, w_screen = [
        piece(own * i, own, (width, width)) for i in range(5)
    ]
    w_hidden = piece(own * 5, own * parts, (width, inner))
    w_return = piece(own * (5 + parts), own * parts, (inner, width))

    def position_major(a):
        return jnp.transpose(a, (2, 0, 1, 3)).reshape(rows, width)

    def shifted(a, first):
        return jnp.concatenate([first, a[:-segs]], 0)

    x = position_major(tokens).astype(f32)
    n1, inv1 = normalise(x)
    one = n1 * mixer_g + mixer_b
    before = shifted(one, entering(one[-segs:], spot))
    spread_one = one - before
    key_in = (before + spread_one * key_share).astype(bf16)
    value_in = (before + spread_one * value_share).astype(bf16)
    gate_in = (before + spread_one * gate_share).astype(bf16)
    k = mm(key_in, w_key).astype(bf16)
    v = mm(value_in, w_value).astype(bf16)
    gate = jax.nn.sigmoid(mm(gate_in, w_gate))

    rate = jnp.exp(decay_log)
    cube = (span, segs, width)
    offsets = jnp.arange(span, dtype=f32)[:, None, None]
    kw = k.reshape(cube).astype(f32)
    vw = v.reshape(cube).astype(f32)
    shifted_key = kw - (span - 1.0 - offsets) * rate
    ends = jnp.exp(shifted_key)
    totals = jnp.stack([jnp.sum(ends * vw, 0), jnp.sum(ends, 0)])
    tops = jnp.max(shifted_key, 0)
    everyone = lax.all_gather(jnp.concatenate([totals, tops[None]]), "seq", axis=0)
    everyone = everyone.reshape(count, 3, groups, stretches, width)
    everyone = jnp.transpose(everyone, (3, 0, 1, 2, 4)).reshape(
        stretches * count, 3, groups, width
    )
    order = jnp.arange(stretches * count, dtype=f32)

    def weights_for(here):
        gap = here - 1.0 - order[:, None]
        return jnp.where(gap >= 0, jnp.exp(-jnp.maximum(gap, 0.0) * (span * rate)), 0.0)

    def carried(here):
        return jnp.sum(weights_for(here)[:, None, None, :] * everyone[:, :2], 0)

    carry = jnp.stack([carried(j * count + spot.astype(f32)) for j in range(stretches)], 2)
    carry = carry.reshape(2, segs, width)
    final = carried(float(stretches * count))
    far = (stretches * count - 1.0 - order)[:, None] * (span * rate)
    top = jnp.max(everyone[:, 2] - far[:, None, :], 0)
    slab = width // count

    def own_slab(a):
        return lax.dynamic_slice_in_dim(a, spot * slab, slab, 1)

    final_top = own_slab(top)
    scaling = jnp.exp(-final_top)
    final_num = own_slab(final[0]) * scaling
    final_den = own_slab(final[1]) * scaling

    num, den, mix_raw = call(
        forward_kernel, [(cube, f32)] * 3, k.reshape(cube), v.reshape(cube), carry,
        decay_log, first_log,
    )
    mix = mix_raw.reshape(rows, width).astype(bf16).astype(f32)
    gated = (gate * mix).astype(bf16)
    residual = x + mm(gated, w_output)
    n2, inv2 = normalise(residual)
    two = n2 * channel_g + channel_b
    before = shifted(two, entering(two[-segs:], spot))
    spread_two = two - before
    hidden_in = (before + spread_two * hidden_share).astype(bf16)
    screen_in = (before + spread_two * screen_share).astype(bf16)
    screen = jax.nn.sigmoid(mm(screen_in, w_screen))
    cot = position_major(cotangent).astype(f32)
    returned_grad = (cot * screen).astype(bf16)
    relu = jnp.maximum(mm(hidden_in, w_hidden), 0.0)
    act = jnp.square(relu).astype(bf16)
    returned = mm(act, w_return)
    output = (residual + screen * returned).astype(bf16)

    screen_grad = (cot * returned * screen * (1.0 - screen)).astype(bf16)
    hidden_grad = (mm_nt(returned_grad, w_return) * (2.0 * relu)).astype(bf16)
    dw_return = mm_tn(act, returned_grad)
    dw_hidden = mm_tn(hidden_in, hidden_grad)
    dw_screen = mm_tn(screen_in, screen_grad)
    hidden_back = mm_nt(hidden_grad, w_hidden)
    screen_back = mm_nt(screen_grad, w_screen)
    d_hidden_blend = jnp.sum(hidden_back * spread_two, 0)
    d_screen_blend = jnp.sum(screen_back * spread_two, 0)
    ahead = hidden_back * (1.0 - hidden_share) + screen_back * (1.0 - screen_share)
    two_grad = (
        hidden_back * hidden_share
        + screen_back * screen_share
        + jnp.concatenate([ahead[segs:], leaving(ahead[:segs], spot)], 0)
    )
    d_channel_gain = jnp.sum(two_grad * n2, 0)
    d_channel_bias = jnp.sum(two_grad, 0)
    residual_grad = cot + norm_back(two_grad, n2, inv2, channel_g)
    output_grad = residual_grad.astype(bf16)
    dw_output = mm_tn(gated, output_grad)
    gated_grad = mm_nt(output_grad, w_output)
    mix_grad = (gated_grad * gate).astype(bf16)
    gate_grad = (gated_grad * mix * gate * (1.0 - gate)).astype(bf16)

    boost = jnp.exp(first_log + kw)
    num_grad = mix_grad.reshape(cube).astype(f32) / (den + boost)
    den_grad = -num_grad * mix_raw
    fade = jnp.exp(-offsets * rate)
    totals = jnp.stack([jnp.sum(fade * num_grad, 0), jnp.sum(fade * den_grad, 0)])
    everyone = lax.all_gather(totals, "seq", axis=0)
    everyone = everyone.reshape(count, 2, groups, stretches, width)
    everyone = jnp.transpose(everyone, (3, 0, 1, 2, 4)).reshape(
        stretches * count, 2, groups, width
    )

    def carried_back(here):
        gap = order[:, None] - here - 1.0
        scale = jnp.where(gap >= 0, jnp.exp(-jnp.maximum(gap, 0.0) * (span * rate)), 0.0)
        return jnp.sum(scale[:, None, None, :] * everyone, 0)

    carry = jnp.stack([carried_back(j * count + spot.astype(f32)) for j in range(stretches)], 2)
    carry = carry.reshape(2, segs, width)
    key_grad, value_grad, first_sum, decay_sum = call(
        backward_kernel, [(cube, bf16)] * 2 + [((segs, width), f32)] * 2,
        k.reshape(cube), v.reshape(cube), num, den, mix_raw, mix_grad.reshape(cube), carry,
        decay_log, first_log,
    )
    key_grad = key_grad.reshape(rows, width)
    value_grad = value_grad.reshape(rows, width)
    d_first = jnp.sum(first_sum, 0)
    d_decay = -rate[0] * jnp.exp(-rate[0]) * jnp.sum(decay_sum, 0)
    dw_key = mm_tn(key_in, key_grad)
    dw_value = mm_tn(value_in, value_grad)
    dw_gate = mm_tn(gate_in, gate_grad)
    key_back = mm_nt(key_grad, w_key)
    value_back = mm_nt(value_grad, w_value)
    gate_back = mm_nt(gate_grad, w_gate)
    d_key_blend = jnp.sum(key_back * spread_one, 0)
    d_value_blend = jnp.sum(value_back * spread_one, 0)
    d_gate_blend = jnp.sum(gate_back * spread_one, 0)
    ahead = (
        key_back * (1.0 - key_share)
        + value_back * (1.0 - value_share)
        + gate_back * (1.0 - gate_share)
    )
    one_grad = (
        key_back * key_share
        + value_back * value_share
        + gate_back * gate_share
        + jnp.concatenate([ahead[segs:], leaving(ahead[:segs], spot)], 0)
    )
    d_mixer_gain = jnp.sum(one_grad * n1, 0)
    d_mixer_bias = jnp.sum(one_grad, 0)
    input_grad = residual_grad + norm_back(one_grad, n1, inv1, mixer_g)

    packed = jnp.concatenate(
        [d.reshape(owners, own, width).astype(bf16) for d in (dw_key, dw_value, dw_gate, dw_output, dw_screen)]
        + [
            dw_hidden.reshape(owners, own * parts, width).astype(bf16),
            dw_return.reshape(owners, own * parts, width).astype(bf16),
        ],
        1,
    )
    summed = lax.psum_scatter(packed, both, scatter_dimension=0).astype(f32)
    small = jnp.stack(
        [
            d_mixer_gain, d_mixer_bias, d_key_blend, d_value_blend, d_gate_blend, d_decay, d_first,
            d_channel_gain, d_channel_bias, d_hidden_blend, d_screen_blend,
        ]
    )
    small = lax.psum(small, both)
    place = (spot * lax.axis_size("rep") + lax.axis_index("rep")) * own
    small = lax.dynamic_slice_in_dim(small, place, own, 1)

    def batch_major(a):
        return jnp.transpose(a.reshape(span, groups, stretches, width), (1, 2, 0, 3))

    return (
        batch_major(output),
        batch_major(input_grad),
        final_num,
        final_den,
        final_top,
        *[small[i] for i in range(7)],
        *[summed[own * i : own * (i + 1)] for i in range(4)],
        *[small[i] for i in range(7, 11)],
        summed[own * 5 : own * (5 + parts)].reshape(own, inner),
        summed[own * 4 : own * 5],
        summed[own * (5 + parts) :],
    )


def solution(mesh):
    rows = P("rep", None, "seq", None)
    owned = P(both)
    owned_rows = P(both, None)
    in_specs = (rows,) + (owned,) * 7 + (owned_rows,) * 4 + (owned,) * 4 + (owned_rows,) * 3 + (rows,)
    out_specs = (
        (rows,) * 2 + (P("rep", "seq"),) * 3 + (owned,) * 7 + (owned_rows,) * 4
        + (owned,) * 4 + (owned_rows,) * 3
    )
    return jax.shard_map(body, mesh=mesh, in_specs=in_specs, out_specs=out_specs, check_vma=False)
```

time: 1670 us -> 614 us (0.37)
  waiting for transfers between devices: 647 us -> 159 us
  matrix products: 349 us -> 98.7 us
  local copies, waits for them, and re-layouts: 389 us -> 156 us
  starting transfers between devices: 79.5 us -> 18.7 us
  other arithmetic: 95.5 us -> 57.3 us
    reduce_scatter x7 -> x1, waiting for transfers between devices: 524 us -> 94.3 us  [body(): summed = lax.psum_scatter(packed, both, scatter_dimension=0).astype(f32)]
    dot_general x54 -> x21, matrix products: 349 us -> 98.7 us  [the longest x7 34.7 us: mm_tn(): lax.dot_general(left, right, (((0,), (0,)), ((), ())), preferred_element_...]
    convert_element_type x48 -> x11, local copies, waits for them, and re-layouts: 172 us -> 40.9 us  [the longest x2 9.77 us: body(): cot = position_major(cotangent).astype(f32)]
    unnamed x515 -> x243, local copies, waits for them, and re-layouts: 115 us -> 23.2 us
    unnamed x2 -> x0, blocking collectives: 82.1 us -> none
    all_to_all x12 -> x0, waiting for transfers between devices: 69 us -> none  [the longest x2 17.1 us: body(): lax.all_to_all(address_segment_derivative.astype(jnp.bfloat16), 'seq', sp...]
    all_to_all x12 -> x0, starting transfers between devices: 62.7 us -> none  [the longest x2 11.5 us: body(): lax.all_to_all(raw_part.astype(jnp.bfloat16), 'seq', split_axis=2, concat...]
    all_gather x0 -> x1, blocking collectives: none -> 44.1 us  [body(): spread_vectors = lax.all_gather(jnp.stack(vectors), both, axis=0)]
  transfers between devices with their start and end apart: 34 -> 8, of which waited for: 19 -> 5; matrix products, arithmetic and copies ran while one was open for 34% -> 27% of each run, Pallas kernels for 0% -> 0%
where the time goes in v1:
time: 614 us; the launch traced here: 605 us
  waiting for transfers between devices  159 us (26%)
  local copies, waits for them, and re-layouts  156 us (25%)
  matrix products  98.7 us (16%)
  blocking collectives  84.5 us (14%)
  other arithmetic  57.3 us (9%)
  starting transfers between devices  18.7 us (3%)
  between operations  15.8 us (3%)
  Pallas kernels  15.3 us (2%)
    reduce_scatter x1, waiting for transfers between devices, body(): summed = lax.psum_scatter(packed, both, scatter_dimension=0).astype(f32)  94.3 us
    all_gather x1, blocking collectives, body(): spread_vectors = lax.all_gather(jnp.stack(vectors), both, axis=0)  44.1 us
    psum x1, blocking collectives, body(): small = lax.psum(small, both)  40.4 us
    dot_general x7, matrix products, mm_tn(): lax.dot_general(left, right, (((0,), (0,)), ((), ())), preferred_element_...  34.7 us
    dot_general x7, matrix products, mm(): return jnp.dot(left, right, preferred_element_type=f32)  32.5 us
    dot_general x7, matrix products, mm_nt(): lax.dot_general(left, right, (((1,), (1,)), ((), ())), preferred_element_...  31.6 us
    all_gather x1, waiting for transfers between devices, body(): lax.all_gather(jnp.concatenate([totals, tops[None]]), 'seq', axis=0)  24.4 us
    all_gather x1, waiting for transfers between devices, body(): everyone = lax.all_gather(totals, 'seq', axis=0)  23.8 us
  transfers between devices with their start and end apart: 8, of which 5 were waited for; matrix products, arithmetic and copies ran while one was open for 27% of the time, Pallas kernels for 0%

profile of v1, /device:TPU:0, one launch (start us, length us, event | category | flops | bytes accessed | tf_op | source)
XLA Modules:
  0.0 605.4 jit_solution(18441851757239102806)
XLA Ops:
  14.1 1.7 fusion.12
  16.2 44.1 %all-gather.4 = bf16[32,11,24]{2,1,0:T(8,128)(2,1)S(1)} all-gather(bf16[1,11,24]{2,1,0:T(8,128)(2,1)S(1)} %bitcast.223), channel_id=2, replica_groups=mesh['seq'=16,'rep'=2] {'seq','rep'}, dimensions={0}, use_global_device_ids=true | all-gather | bytes 17424 | tf_op jit(solution)/shard_map/all_gather | solution.py:139
  60.3 1.9 subtract_reduce_fusion.2
  63.9 4.1 copy.104
  68.0 3.9 reshape.738
  74.2 9.9 %collective-permute-start = (f32[16,768]{1,0:T(8,128)}, f32[16,768]{1,0:T(8,128)}, u32[]{:S(2)}, u32[]{:S(2)}) collective-permute-start(f32[16,768]{1,0:T(8,128)} %slice.254), channel_id=1, source_target_pairs={{0,2},{2,4},{4,6},{6,8},{8,10},{10,12},{12,14},{14,16},{16,18},{18... | collective-permute-start | bytes 147464 | tf_op jit(solution)/shard_map/ppermute | solution.py:40
  85.6 2.1 slice.256
  90.0 3.5 collective-permute-done
  95.8 1.9 pad_maximum_fusion
  97.7 5.2 concatenate.37
  102.9 4.8 add_convert_fusion.6
  113.2 13.4 %all-gather.9.cloned.1.call-done = bf16[9984,768]{1,0:T(8,128)(2,1)} async-done(((bf16[312,768]{1,0:T(8,128)(2,1)}), bf16[9984,768]{1,0:T(8,128)(2,1)}) %all-gather.9.cloned.1.call-update) | async-done | bytes 15335440 | tf_op jit(solution)/shard_map/all_gather | solution.py:138
  126.6 4.6 fusion.47
  150.2 1.7 convert_bitcast_fusion
  151.9 4.1 copy.120
  156.0 5.7 reshape.740
  164.1 4.2 copy.113
  168.3 4.6 convert_element_type.165
  172.9 24.4 %all-gather.11.cloned.1.call-done = f32[48,16,768]{2,1,0:T(8,128)} async-done(((f32[3,16,768]{2,1,0:T(8,128)}), f32[48,16,768]{2,1,0:T(8,128)}) %all-gather.11.cloned.1.call-update) | async-done | bytes 2359312 | tf_op jit(solution)/shard_map/all_gather | solution.py:182
  197.3 4.0 reshape.717
  201.3 1.9 copy.118
  204.8 6.0 shard_map.371
  210.8 5.4 fusion.8
  223.7 7.9 %fusion.46 = (bf16[32,96,768]{2,1,0:T(8,128)(2,1)}, bf16[32,96,768]{2,1,0:T(8,128)(2,1)}) fusion(bf16[32,312,768]{2,1,0:T(8,128)(2,1)} %bitcast.185), kind=kLoop, calls=%fused_computation.200 | loop fusion | bytes 18874368 | tf_op jit(solution)/shard_map/slice | solution.py:147
  231.6 8.6 %reshape.724 = bf16[768,3072]{1,0:T(8,128)(2,1)} reshape(bf16[32,96,768]{2,1,0:T(8,128)(2,1)} %get-tuple-element.82) | data formatting | bytes 9437184 | tf_op jit(solution)/shard_map/reshape | solution.py:147
  240.2 3.8 slice.271
  244.2 3.7 add_convert_fusion.4
  247.9 10.9 %fusion.50 = f32[1024,3072]{1,0:T(8,128)} fusion(bf16[1024,768]{1,0:T(8,128)(2,1)S(1)} %get-tuple-element.99, bf16[768,3072]{1,0:T(8,128)(2,1)} %reshape.724), kind=kOutput, calls=%fused_computation.204 | convolution fusion | flops 4831838208 | bytes 18874368 | tf_op jit(solution)/shard_map/dot_general | solution.py:15
  258.8 8.4 %fusion.14 = f32[1024,768]{1,0:T(8,128)S(1)} fusion(bf16[3072,768]{1,0:T(8,128)(2,1)S(1)} %bitcast.200, f32[1024,3072]{1,0:T(8,128)} %fusion.50), kind=kOutput, calls=%fused_computation.71 | convolution fusion | flops 4841275392 | bytes 20447232 | tf_op jit(solution)/shard_map/dot_general | solution.py:15
  267.3 3.4 multiply_convert_fusion.4
  270.7 11.0 %multiply_convert_fusion = bf16[1024,3072]{1,0:T(8,128)(2,1)} fusion(f32[1024,3072]{1,0:T(8,128)} %fusion.50, bf16[1024,768]{1,0:T(8,128)(2,1)S(1)} %get-tuple-element.96, bf16[3072,768]{1,0:T(8,128)(2,1)S(1)} %bitcast.201), kind=kOutput, calls=%fused_computation | convolution fusion | flops 4844421120 | bytes 25165824 | tf_op jit(solution)/shard_map/dot_general | solution.py:19
  281.8 7.6 %fusion.51 = f32[1024,768]{1,0:T(8,128)S(1)} fusion(bf16[1024,3072]{1,0:T(8,128)(2,1)} %multiply_convert_fusion, bf16[768,3072]{1,0:T(8,128)(2,1)S(1)} %bitcast.197), kind=kOutput, calls=%fused_computation.205 | convolution fusion | flops 4831838208 | bytes 14155776 | tf_op jit(solution)/shard_map/dot_general | solution.py:19
  289.5 4.2 multiply_reduce_fusion
  293.7 4.2 collective-permute-start.2
  297.9 6.9 %convolution_convert_fusion.1 = bf16[768,3072]{1,0:T(8,128)(2,1)} fusion(bf16[1024,768]{1,0:T(8,128)(2,1)S(1)} %get-tuple-element.99, bf16[1024,3072]{1,0:T(8,128)(2,1)S(1)} %copy-done.106), kind=kOutput, calls=%fused_computation.3 | convolution fusion | flops 4834197504 | bytes 12582912 | tf_op jit(solution)/shard_map/dot_general | solution.py:23
  304.7 1.8 slice.277
  306.7 6.6 %multiply_reduce_fusion.2 = (f32[768]{0:T(1024)}, f32[1024]{0:T(1024)S(1)}, f32[1024]{0:T(1024)S(1)}, f32[768]{0:T(1024)}, f32[1024,768]{1,0:T(8,128)S(1)}) fusion(f32[1024,768]{1,0:T(8,128)} %copy-done.5, f32[1024]{0:T(1024)S(1)} %add_rsqrt_fusion, f32[1024]{0:T(1024)S(1)} %broadcast_multiply_fusion.6, f32[768]{0:T(1024)S(1)} %mul.574, ...), kind=kLoop, calls=%fused_computation.32 | loop fusion | flops 11006464 | bytes 15760384 | tf_op jit(solution)/shard_map/reduce_sum | solution.py:247
  315.7 1.9 copy-done.36
  317.7 2.8 multiply_convert_fusion.2
  323.3 3.9 convolution_convert_fusion.4
  327.2 9.0 %convert_element_type.204 = bf16[32,96,768]{2,1,0:T(8,128)(2,1)} reshape(bf16[768,3072]{1,0:T(8,128)(2,1)} %convolution_convert_fusion.1) | data formatting | bytes 9437184 | tf_op jit(solution)/shard_map/convert_element_type | solution.py:310
  336.2 12.2 %convolution_convert_fusion = bf16[3072,768]{1,0:T(8,128)(2,1)} fusion(bf16[1024,768]{1,0:T(8,128)(2,1)S(1)} %copy-done.108, f32[1024,3072]{1,0:T(8,128)} %fusion.50), kind=kOutput, calls=%fused_computation.2 | convolution fusion | flops 4843634688 | bytes 18874368 | tf_op jit(solution)/shard_map/dot_general | solution.py:23
  348.4 3.1 fusion.54
  351.6 2.5 convolution_convert_fusion.5
  354.1 23.8 %all-gather.13.cloned.1.call-done = f32[32,16,768]{2,1,0:T(8,128)} async-done(((f32[2,16,768]{2,1,0:T(8,128)}), f32[32,16,768]{2,1,0:T(8,128)}) %all-gather.13.cloned.1.call-update) | async-done | bytes 1572880 | tf_op jit(solution)/shard_map/all_gather | solution.py:261
  377.9 2.2 reshape.730
  381.8 9.3 %shard_map.372 = (bf16[64,16,768]{2,1,0:T(8,128)(2,1)S(1)}, bf16[64,16,768]{2,1,0:T(8,128)(2,1)S(1)}, f32[16,768]{1,0:T(8,128)S(1)}, f32[16,768]{1,0:T(8,128)S(1)}) custom-call(bf16[64,16,768]{2,1,0:T(8,128)(2,1)S(1)} %bitcast.174, bf16[64,16,768]{2,1,0:T(8,128)(2,1)} %bitcast.177, f32[64,16,768]{2,1,0:T(8,128)} %get-tuple-element.31.num_ref, ...), custom_call_target="tpu_custom_call" | custom-call | tf_op jit(solution)/shard_map/pallas_call | solution.py:106
  397.6 6.2 %multiply_reduce_fusion.3 = (f32[768]{0:T(1024)S(1)}, f32[768]{0:T(1024)S(1)}, f32[768]{0:T(1024)S(1)}, f32[1024,768]{1,0:T(8,128)}, bf16[768,1024]{0,1:T(8,128)...) fusion(f32[1024,768]{1,0:T(8,128)S(1)} %copy-done.28, f32[1008,768]{1,0:T(8,128)S(1)} %copy-done.19, ...), kind=kLoop, calls=%fused_computation.33 | loop fusion | flops 20444928 | bytes 23634944 | tf_op jit(solution)/shard_map/reduce_sum | solution.py:291
  403.8 1.8 copy.124
  405.5 2.7 copy.123
  408.3 1.7 copy.122
  409.9 4.0 fusion.29
  414.0 2.6 fusion.28
  416.6 2.6 fusion.25
  421.5 2.5 constant_dynamic-update-slice_fusion.8
  424.0 2.5 constant_dynamic-update-slice_fusion.7
  433.2 3.0 collective-permute-start.3
  436.3 3.9 slice.280
  440.4 8.4 %multiply_reduce_fusion.6 = (f32[768]{0:T(1024)S(1)}, f32[1024]{0:T(1024)S(1)}, f32[1024]{0:T(1024)S(1)}, f32[768]{0:T(1024)S(1)}, f32[1024,768]{1,0:T(8,128)S(1)}) fusion(f32[1024,768]{1,0:T(8,128)} %copy-done.8, f32[1024]{0:T(1024)S(1)} %copy-done.66, f32[1024]{0:T(1024)S(1)} %copy-done.68, f32[768]{0:T(1024)S(1)} %copy-done.64, ...), kind=kLoop, calls=%fused_computation.36 | loop fusion | flops 12579328 | bytes 18909184 | tf_op jit(solution)/shard_map/reduce_sum | solution.py:303
  449.3 2.3 multiply_add_fusion
  451.6 3.8 reshape.736
  455.4 3.5 copy.136
  459.0 40.4 %psum.7 = f32[11,768]{1,0:T(8,128)S(1)} all-reduce(f32[11,768]{1,0:T(8,128)S(1)} %stack.136), channel_id=1, replica_groups=mesh['seq'=16,'rep'=2] {'seq','rep'}, use_global_device_ids=true, to_apply=%region_30.31 | all-reduce | flops 8448 | bytes 67584 | tf_op jit(solution)/shard_map/psum | solution.py:322
  500.0 94.3 %reduce-scatter.2.cloned.1.call-done = bf16[1,312,768]{2,1,0:T(8,128)(2,1)} async-done(((bf16[32,312,768]{2,1,0:T(8,128)(2,1)}), bf16[1,312,768]{2,1,0:T(8,128)(2,1)}) %reduce-scatter.2.cloned.1.call-update) | async-done | bytes 479248 | tf_op jit(solution)/shard_map/reduce_scatter | solution.py:315
  (379 shorter events, 80.7 us)
Async XLA Ops:
  7.2 55.2 %copy-start.21 = (bf16[8,2,64,768]{3,2,1,0:T(8,128)(2,1)S(1)}, bf16[8,2,64,768]{3,2,1,0:T(8,128)(2,1)}, u32[]{:S(2)}) copy-start(bf16[8,2,64,768]{3,2,1,0:T(8,128)(2,1)} %param.20) | copy-start | bytes 4718596
  7.2 8.8 %copy-start.103 = (bf16[24]{0:T(256)(128)(2,1)S(1)}, bf16[24]{0:T(256)(128)(2,1)}, u32[]{:S(2)}) copy-start(bf16[24]{0:T(256)(128)(2,1)} %param.35) | copy-start | bytes 148
  7.2 8.8 %copy-start.102 = (bf16[24]{0:T(256)(128)(2,1)S(1)}, bf16[24]{0:T(256)(128)(2,1)}, u32[]{:S(2)}) copy-start(bf16[24]{0:T(256)(128)(2,1)} %param.34) | copy-start | bytes 148
  7.2 8.8 %copy-start.101 = (bf16[24]{0:T(256)(128)(2,1)S(1)}, bf16[24]{0:T(256)(128)(2,1)}, u32[]{:S(2)}) copy-start(bf16[24]{0:T(256)(128)(2,1)} %param.33) | copy-start | bytes 148
  7.2 8.8 %copy-start.100 = (bf16[24]{0:T(256)(128)(2,1)S(1)}, bf16[24]{0:T(256)(128)(2,1)}, u32[]{:S(2)}) copy-start(bf16[24]{0:T(256)(128)(2,1)} %param.32) | copy-start | bytes 148
  7.2 8.8 %copy-start.99 = (bf16[24]{0:T(256)(128)(2,1)S(1)}, bf16[24]{0:T(256)(128)(2,1)}, u32[]{:S(2)}) copy-start(bf16[24]{0:T(256)(128)(2,1)} %param.27) | copy-start | bytes 148
  7.3 8.8 %copy-start.98 = (bf16[24]{0:T(256)(128)(2,1)S(1)}, bf16[24]{0:T(256)(128)(2,1)}, u32[]{:S(2)}) copy-start(bf16[24]{0:T(256)(128)(2,1)} %param.26) | copy-start | bytes 148
  7.3 8.8 %copy-start.97 = (bf16[24]{0:T(256)(128)(2,1)S(1)}, bf16[24]{0:T(256)(128)(2,1)}, u32[]{:S(2)}) copy-start(bf16[24]{0:T(256)(128)(2,1)} %param.25) | copy-start | bytes 148
  7.3 8.8 %copy-start.96 = (bf16[24]{0:T(256)(128)(2,1)S(1)}, bf16[24]{0:T(256)(128)(2,1)}, u32[]{:S(2)}) copy-start(bf16[24]{0:T(256)(128)(2,1)} %param.24) | copy-start | bytes 148
  7.3 8.8 %copy-start.95 = (bf16[24]{0:T(256)(128)(2,1)S(1)}, bf16[24]{0:T(256)(128)(2,1)}, u32[]{:S(2)}) copy-start(bf16[24]{0:T(256)(128)(2,1)} %param.23) | copy-start | bytes 148
  7.3 8.8 %copy-start.94 = (bf16[24]{0:T(256)(128)(2,1)S(1)}, bf16[24]{0:T(256)(128)(2,1)}, u32[]{:S(2)}) copy-start(bf16[24]{0:T(256)(128)(2,1)} %param.22) | copy-start | bytes 148
  7.3 8.8 %copy-start.93 = (bf16[24]{0:T(256)(128)(2,1)S(1)}, bf16[24]{0:T(256)(128)(2,1)}, u32[]{:S(2)}) copy-start(bf16[24]{0:T(256)(128)(2,1)} %param.21) | copy-start | bytes 148
  7.3 119.3 %all-gather.9.cloned.1.call-start = ((), (), s32[]{:S(2)}) async-start(), calls=%async_computation.2 | async-start | bytes 15814656 | tf_op jit(solution)/shard_map/all_gather | solution.py:138
  14.1 183.2 %all-gather.11.cloned.1.call-start = ((), (), s32[]{:S(2)}) async-start(), calls=%async_computation.3 | async-start | bytes 2506752 | tf_op jit(solution)/shard_map/all_gather | solution.py:182
  15.8 47.1 %copy-start.69 = (f32[64,8,2]{0,2,1:T(2,128)}, f32[64,8,2]{0,2,1:T(2,128)S(1)}, u32[]{:S(2)}) copy-start(f32[64,8,2]{0,2,1:T(2,128)S(1)} %copy.107) | copy-start | bytes 12292
  62.3 40.6 %copy-start.63 = (f32[768]{0:T(1024)}, f32[768]{0:T(1024)S(1)}, u32[]{:S(2)}) copy-start(f32[768]{0:T(1024)S(1)} %mul.538) | copy-start | bytes 9220
  62.4 9.5 %copy-start.77 = (f32[768]{0:T(1024)}, f32[768]{0:T(1024)S(1)}, u32[]{:S(2)}) copy-start(f32[768]{0:T(1024)S(1)} %add.182) | copy-start | bytes 9220
  63.3 8.6 %copy-start.65 = (f32[1024]{0:T(1024)}, f32[1024]{0:T(1024)S(1)}, u32[]{:S(2)}) copy-start(f32[1024]{0:T(1024)S(1)} %rsqrt.21) | copy-start | bytes 12292
  63.5 8.4 %copy-start.67 = (f32[1024]{0:T(1024)}, f32[1024]{0:T(1024)S(1)}, u32[]{:S(2)}) copy-start(f32[1024]{0:T(1024)S(1)} %div.36) | copy-start | bytes 12292
  73.6 10.6 %copy-start.23 = (f32[1024,768]{1,0:T(8,128)}, f32[1024,768]{1,0:T(8,128)S(1)}, u32[]{:S(2)}) copy-start(f32[1024,768]{1,0:T(8,128)S(1)} %multiply_add_fusion.5) | copy-start | bytes 9437188
  74.2 19.3 %collective-permute-start = (f32[16,768]{1,0:T(8,128)}, f32[16,768]{1,0:T(8,128)}, u32[]{:S(2)}, u32[]{:S(2)}) collective-permute-start(f32[16,768]{1,0:T(8,128)} %slice.254), channel_id=1, source_target_pairs={{0,2},{2,4},{4,6},{6,8},{8,10},{10,12},{12,14},{14,16},{16,18},{18... | collective-permute-start | bytes 147464 | tf_op jit(solution)/shard_map/ppermute | solution.py:40
  87.7 20.1 %copy-start.18 = (f32[1008,768]{1,0:T(8,128)}, f32[1008,768]{1,0:T(8,128)S(1)}, u32[]{:S(2)}) copy-start(f32[1008,768]{1,0:T(8,128)S(1)} %slice.256) | copy-start | bytes 9289732
  95.8 7.1 %copy-start.56 = (f32[16,768]{1,0:T(8,128)}, f32[16,768]{1,0:T(8,128)S(1)}, u32[]{:S(2)}) copy-start(f32[16,768]{1,0:T(8,128)S(1)} %reshape.710) | copy-start | bytes 147460
  97.7 5.2 copy-start.70
  134.9 69.9 %copy-start = (bf16[1024,768]{1,0:T(8,128)(2,1)}, bf16[1024,768]{1,0:T(8,128)(2,1)S(1)}, u32[]{:S(2)}) copy-start(bf16[1024,768]{1,0:T(8,128)(2,1)S(1)} %convolution_convert_fusion.2) | copy-start | bytes 4718596
  136.5 241.4 %all-gather.13.cloned.1.call-start = ((), (), s32[]{:S(2)}) async-start(), calls=%async_computation.4 | async-start | bytes 1671168 | tf_op jit(solution)/shard_map/all_gather | solution.py:261
  156.0 5.8 copy-start.81
  204.8 6.0 copy-start.38
  204.8 6.0 copy-start.51
  210.8 6.5 %copy-start.9 = (f32[1024,768]{1,0:T(8,128)S(1)}, f32[1024,768]{1,0:T(8,128)}, u32[]{:S(2)}) copy-start(f32[1024,768]{1,0:T(8,128)} %copy-done.8) | copy-start | bytes 9437188
  210.8 6.5 %copy-start.33 = (bf16[32,24,768]{2,1,0:T(8,128)(2,1)S(1)}, bf16[32,24,768]{2,1,0:T(8,128)(2,1)}, u32[]{:S(2)}) copy-start(bf16[32,24,768]{2,1,0:T(8,128)(2,1)} %get-tuple-element.85) | copy-start | bytes 3538948
  222.2 21.8 %collective-permute-start.1 = (f32[16,768]{1,0:T(8,128)S(1)}, f32[16,768]{1,0:T(8,128)S(1)}, u32[]{:S(2)}, u32[]{:S(2)}) collective-permute-start(f32[16,768]{1,0:T(8,128)S(1)} %slice.269), channel_id=1, source_target_pairs={{0,2},{2,4},{4,6},{6,8},{8,10},{10,12},{12,14},{14,16},{16,18},{18... | collective-permute-start | bytes 147464 | tf_op jit(solution)/shard_map/ppermute | solution.py:40
  244.2 14.6 %slice-start.6 = ((s8[4718592]{0:T(1024)(128)(4,1)}), s8[4194304]{0:T(1024)(128)(4,1)S(1)}, s32[]{:S(2)}) async-start(s8[4718592]{0:T(1024)(128)(4,1)} %bitcast.198), calls=%async_computation.11 | async-start | bytes 8388608
  247.9 19.4 %copy-start.44 = (bf16[1024,768]{1,0:T(8,128)(2,1)}, bf16[1024,768]{1,0:T(8,128)(2,1)S(1)}, u32[]{:S(2)}) copy-start(bf16[1024,768]{1,0:T(8,128)(2,1)S(1)} %get-tuple-element.100) | copy-start | bytes 4718596
  247.9 10.9 %slice-start.7 = ((s8[4718592]{0:T(1024)(128)(4,1)}), s8[524288]{0:T(1024)(128)(4,1)S(1)}, s32[]{:S(2)}) async-start(s8[4718592]{0:T(1024)(128)(4,1)} %bitcast.198), calls=%async_computation.12 | async-start | bytes 1048576
  258.8 8.5 %copy-start.6 = (f32[1024,768]{1,0:T(8,128)S(1)}, f32[1024,768]{1,0:T(8,128)}, u32[]{:S(2)}) copy-start(f32[1024,768]{1,0:T(8,128)} %copy-done.5) | copy-start | bytes 9437188
  258.8 8.5 %copy-start.24 = (f32[1024,768]{1,0:T(8,128)S(1)}, f32[1024,768]{1,0:T(8,128)}, u32[]{:S(2)}) copy-start(f32[1024,768]{1,0:T(8,128)} %reshape.740) | copy-start | bytes 9437188
  258.8 8.5 %copy-start.35 = (bf16[32,24,768]{2,1,0:T(8,128)(2,1)S(1)}, bf16[32,24,768]{2,1,0:T(8,128)(2,1)}, u32[]{:S(2)}) copy-start(bf16[32,24,768]{2,1,0:T(8,128)(2,1)} %get-tuple-element.84) | copy-start | bytes 3538948
  267.3 14.5 %slice-start.4 = ((s8[4718592]{0:T(1024)(128)(4,1)}), s8[4194304]{0:T(1024)(128)(4,1)S(1)}, s32[]{:S(2)}) async-start(s8[4718592]{0:T(1024)(128)(4,1)} %bitcast.196), calls=%async_computation.9 | async-start | bytes 8388608
  270.7 11.0 %copy-start.107 = (bf16[1024,768]{1,0:T(8,128)(2,1)}, bf16[1024,768]{1,0:T(8,128)(2,1)S(1)}, u32[]{:S(2)}) copy-start(bf16[1024,768]{1,0:T(8,128)(2,1)S(1)} %get-tuple-element.96) | copy-start | bytes 4718596
  270.7 18.7 %copy-start.46 = (bf16[1024,768]{1,0:T(8,128)(2,1)}, bf16[1024,768]{1,0:T(8,128)(2,1)S(1)}, u32[]{:S(2)}) copy-start(bf16[1024,768]{1,0:T(8,128)(2,1)S(1)} %get-tuple-element.97) | copy-start | bytes 4718596
  270.7 11.0 %slice-start.5 = ((s8[4718592]{0:T(1024)(128)(4,1)}), s8[524288]{0:T(1024)(128)(4,1)S(1)}, s32[]{:S(2)}) async-start(s8[4718592]{0:T(1024)(128)(4,1)} %bitcast.196), calls=%async_computation.10 | async-start | bytes 1048576
  281.8 7.7 %copy-start.17 = (f32[1024,768]{1,0:T(8,128)S(1)}, f32[1024,768]{1,0:T(8,128)}, u32[]{:S(2)}) copy-start(f32[1024,768]{1,0:T(8,128)} %copy-done.16) | copy-start | bytes 9437188
  281.8 7.7 %copy-start.20 = (f32[1008,768]{1,0:T(8,128)S(1)}, f32[1008,768]{1,0:T(8,128)}, u32[]{:S(2)}) copy-start(f32[1008,768]{1,0:T(8,128)} %slice.271) | copy-start | bytes 9289732
  281.8 7.7 %copy-start.89 = (f32[768]{0:T(1024)S(1)}, f32[768]{0:T(1024)}, u32[]{:S(2)}) copy-start(f32[768]{0:T(1024)} %mul.596) | copy-start | bytes 9220
  281.8 7.7 %copy-start.90 = (f32[768]{0:T(1024)S(1)}, f32[768]{0:T(1024)}, u32[]{:S(2)}) copy-start(f32[768]{0:T(1024)} %mul.593) | copy-start | bytes 9220
  289.5 8.3 %copy-start.106 = (bf16[1024,3072]{1,0:T(8,128)(2,1)S(1)}, bf16[1024,3072]{1,0:T(8,128)(2,1)}, u32[]{:S(2)}) copy-start(bf16[1024,3072]{1,0:T(8,128)(2,1)} %multiply_convert_fusion) | copy-start | bytes 18874372
  293.7 12.8 %collective-permute-start.2 = (f32[16,768]{1,0:T(8,128)S(1)}, f32[16,768]{1,0:T(8,128)S(1)}, u32[]{:S(2)}, u32[]{:S(2)}) collective-permute-start(f32[16,768]{1,0:T(8,128)S(1)} %slice.278), channel_id=1, source_target_pairs={{0,30},{2,0},{4,2},{6,4},{8,6},{10,8},{12,10},{14,12},{16,14},{18,... | collective-permute-start | bytes 147464 | tf_op jit(solution)/shard_map/ppermute | solution.py:40
  306.7 6.6 %copy-start.7 = (f32[1024,768]{1,0:T(8,128)S(1)}, f32[1024,768]{1,0:T(8,128)}, u32[]{:S(2)}) copy-start(f32[1024,768]{1,0:T(8,128)} %copy-done.5) | copy-start | bytes 9437188
  306.7 6.6 %copy-start.25 = (f32[1024,768]{1,0:T(8,128)S(1)}, f32[1024,768]{1,0:T(8,128)}, u32[]{:S(2)}) copy-start(f32[1024,768]{1,0:T(8,128)} %reshape.740) | copy-start | bytes 9437188
  314.5 6.0 copy-start.12
  323.3 271.0 %reduce-scatter.2.cloned.1.call-start = ((), (), s32[]{:S(2)}) async-start(), calls=%async_computation.1 | async-start | bytes 15814656 | tf_op jit(solution)/shard_map/reduce_scatter | solution.py:315
  327.2 9.0 %copy-start.108 = (bf16[1024,768]{1,0:T(8,128)(2,1)S(1)}, bf16[1024,768]{1,0:T(8,128)(2,1)}, u32[]{:S(2)}) copy-start(bf16[1024,768]{1,0:T(8,128)(2,1)} %copy-done.107) | copy-start | bytes 4718596
  336.2 12.2 %copy-start.42 = (bf16[1024,768]{1,0:T(8,128)(2,1)S(1)}, bf16[1024,768]{1,0:T(8,128)(2,1)}, u32[]{:S(2)}) copy-start(bf16[1024,768]{1,0:T(8,128)(2,1)} %get-tuple-element.95) | copy-start | bytes 4718596
  336.2 12.2 %copy-start.52 = (bf16[32,24,768]{2,1,0:T(8,128)(2,1)S(1)}, bf16[32,24,768]{2,1,0:T(8,128)(2,1)}, u32[]{:S(2)}) copy-start(bf16[32,24,768]{2,1,0:T(8,128)(2,1)} %get-tuple-element.88) | copy-start | bytes 3538948
  354.1 26.1 %copy-start.58 = (f32[2,16,768]{2,0,1:T(2,128)S(1)}, f32[2,16,768]{2,0,1:T(2,128)}, u32[]{:S(2)}) copy-start(f32[2,16,768]{2,0,1:T(2,128)} %get-tuple-element.127) | copy-start | bytes 294916
  354.1 26.1 %copy-start.59 = (f32[2,16,768]{2,0,1:T(2,128)S(1)}, f32[2,16,768]{2,0,1:T(2,128)}, u32[]{:S(2)}) copy-start(f32[2,16,768]{2,0,1:T(2,128)} %get-tuple-element.128) | copy-start | bytes 294916
  381.8 9.4 %copy-start.50 = (bf16[32,24,768]{2,1,0:T(8,128)(2,1)S(1)}, bf16[32,24,768]{2,1,0:T(8,128)(2,1)}, u32[]{:S(2)}) copy-start(bf16[32,24,768]{2,1,0:T(8,128)(2,1)} %copy-done.49) | copy-start | bytes 3538948
  397.6 6.2 %copy-start.30 = (f32[1024,768]{1,0:T(8,128)}, f32[1024,768]{1,0:T(8,128)S(1)}, u32[]{:S(2)}) copy-start(f32[1024,768]{1,0:T(8,128)S(1)} %fusion.52) | copy-start | bytes 9437188
  416.6 5.0 slice-start
  416.6 4.9 slice-start.1
  433.2 7.0 %collective-permute-start.3 = (f32[16,768]{1,0:T(8,128)S(1)}, f32[16,768]{1,0:T(8,128)S(1)}, u32[]{:S(2)}, u32[]{:S(2)}) collective-permute-start(f32[16,768]{1,0:T(8,128)S(1)} %slice.281), channel_id=1, source_target_pairs={{0,30},{2,0},{4,2},{6,4},{8,6},{10,8},{12,10},{14,12},{16,14},{18,... | collective-permute-start | bytes 147464 | tf_op jit(solution)/shard_map/ppermute | solution.py:40
  440.4 8.4 %copy-start.11 = (f32[1024,768]{1,0:T(8,128)S(1)}, f32[1024,768]{1,0:T(8,128)}, u32[]{:S(2)}) copy-start(f32[1024,768]{1,0:T(8,128)} %copy-done.8) | copy-start | bytes 9437188
  440.4 8.9 %copy-start.14 = (f32[1024,768]{1,0:T(8,128)S(1)}, f32[1024,768]{1,0:T(8,128)}, u32[]{:S(2)}) copy-start(f32[1024,768]{1,0:T(8,128)} %copy-done.12) | copy-start | bytes 9437188
  (61 other events, 172.4 us)
Sparse Core Ops, SparseCore 0:
  14.2 112.3 all-gather.8
  136.7 60.6 all-gather.10
  323.4 54.4 all-gather.12
  426.7 167.5 reduce-scatter.1

commit v2 on v1

--- a/solution.py
+++ b/solution.py
@@ -1,3 +1,5 @@
+import functools
+
 import jax
 import jax.numpy as jnp
 from jax import lax
@@ -9,18 +11,31 @@
 bf16 = jnp.bfloat16
 norm_eps = 1e-05
 both = ("seq", "rep")
-
-
-def mm(left, right):
+MESH = pl.DeviceIdType.MESH
+
+KEY, VALUE, GATE, OUTPUT, SCREEN, FIRST_PART = 0, 1, 2, 3, 4, 5
+GROUPS = ((0, 2), (2, 5), (5, 7), (7, 9), (9, 11), (11, 13))
+VECTORS = 11
+(
+    MIXER_G, MIXER_B, KEY_SHARE, VALUE_SHARE, GATE_SHARE, DECAY, FIRST,
+    CHANNEL_G, CHANNEL_B, HIDDEN_SHARE, SCREEN_SHARE,
+) = range(VECTORS)
+
+
+def dot(left, right):
     return jnp.dot(left, right, preferred_element_type=f32)
 
 
-def mm_nt(left, right):
+def dot_nt(left, right):
     return lax.dot_general(left, right, (((1,), (1,)), ((), ())), preferred_element_type=f32)
 
 
-def mm_tn(left, right):
+def dot_tn(left, right):
     return lax.dot_general(left, right, (((0,), (0,)), ((), ())), preferred_element_type=f32)
+
+
+def sigmoid(a):
+    return 1.0 / (1.0 + jnp.exp(-a))
 
 
 def normalise(values):
@@ -33,6 +48,580 @@
     inner = upstream * gain
     centred = inner - jnp.mean(inner, -1, keepdims=True)
     return inverse * (centred - scaled * jnp.mean(inner * scaled, -1, keepdims=True))
+
+
+class Shape:
+    def __init__(self, count, span, groups, stretches, width, inner):
+        self.count, self.span, self.groups, self.stretches = count, span, groups, stretches
+        self.width, self.inner = width, inner
+        self.segs = groups * stretches
+        self.rows = span * self.segs
+        self.depth = count // 4
+        self.chip = width // count
+        self.own = self.chip // 2
+        self.parts = inner // width
+        self.mats = FIRST_PART + 2 * self.parts
+        self.half = width // 2
+
+    def fits(self):
+        return (
+            self.count % 4 == 0 and self.chip % 16 == 0 and self.own % 8 == 0 and self.own <= 32
+            and self.half % 128 == 0 and self.groups == 8 and self.stretches == 2
+            and self.parts == 4 and self.inner % self.width == 0 and self.rows <= 1024
+        )
+
+
+class Place:
+    def __init__(self, sh):
+        self.sh = sh
+        self.s = lax.axis_index("seq")
+        self.r = lax.axis_index("rep")
+        self.z = self.s // 4
+        self.y = lax.rem(self.s // 2, 2)
+        self.x = lax.rem(self.s, 2)
+
+    def device(self, z, y, x, r):
+        return ((z * 2 + y) * 2 + x, r)
+
+    def sibling(self):
+        return (self.s, 1 - self.r)
+
+    def x_peer(self):
+        return self.device(self.z, self.y, 1 - self.x, self.r)
+
+    def y_peer(self):
+        return self.device(self.z, 1 - self.y, self.x, self.r)
+
+    def z_to(self, j):
+        return lax.rem(self.z + 1 + j, self.sh.depth)
+
+    def z_from(self, j):
+        return lax.rem(self.z + self.sh.depth - 1 - j, self.sh.depth)
+
+    def z_peer(self, j):
+        return self.device(self.z_to(j), self.y, self.x, self.r)
+
+    def ring(self, step):
+        count = self.sh.count
+        return (lax.rem(self.s + count + step, count), self.r)
+
+    def a_peer(self):
+        flip_y, flip_x = 1 - self.r, self.r
+        y = self.y + flip_y * (1 - 2 * self.y)
+        x = self.x + flip_x * (1 - 2 * self.x)
+        return self.device(self.z, y, x, self.r)
+
+    def b_peer(self):
+        flip_y, flip_x = self.r, 1 - self.r
+        y = self.y + flip_y * (1 - 2 * self.y)
+        x = self.x + flip_x * (1 - 2 * self.x)
+        return self.device(self.z, y, x, self.r)
+
+    def columns(self, r):
+        half = self.sh.half
+        return pl.ds(pl.multiple_of(r * half, half), half)
+
+
+def send(src, dst, sems, index, device):
+    return pltpu.make_async_remote_copy(
+        src_ref=src, dst_ref=dst, send_sem=sems[0].at[index], recv_sem=sems[1].at[index],
+        device_id=device, device_id_type=MESH,
+    )
+
+
+class Gather:
+    def __init__(self, at, buf, lead, sems, group):
+        self.at, self.buf, self.lead, self.sems, self.group = at, buf, lead, sems, group
+        self.mine = at.columns(at.r)
+
+    def cut(self, z, y, x):
+        return self.buf.at[self.lead + (z, y, x, slice(None), self.mine)]
+
+    def z_copy(self, j):
+        at = self.at
+        block = self.cut(at.z, at.y, at.x)
+        return send(block, block, self.sems, (self.group, j), at.z_peer(j))
+
+    def a_copy(self):
+        at = self.at
+        block = self.cut(slice(None), at.y, at.x)
+        return send(block, block, self.sems, (self.group, at.sh.depth - 1), at.a_peer())
+
+    def b_copy(self, core):
+        at = self.at
+        block = self.cut(slice(None), slice(None), at.x) if core == 0 else self.cut(
+            slice(None), at.y, slice(None)
+        )
+        return send(block, block, self.sems, (self.group, at.sh.depth), at.b_peer())
+
+    def core_copy(self):
+        at = self.at
+        block = self.cut(slice(None), slice(None), slice(None))
+        return send(block, block, self.sems, (self.group, at.sh.depth + 1), at.sibling())
+
+    def z_start(self):
+        for j in range(self.at.sh.depth - 1):
+            self.z_copy(j).start()
+
+    def z_wait(self):
+        for j in range(self.at.sh.depth - 1):
+            self.z_copy(j).wait_recv()
+
+    def a_start(self):
+        self.a_copy().start()
+
+    def a_wait(self):
+        self.a_copy().wait_recv()
+
+    def b_start(self):
+        for core in range(2):
+            @pl.when(self.at.r == core)
+            def _():
+                self.b_copy(core).start()
+
+    def b_wait(self):
+        self.b_copy(0).wait_recv()
+
+    def core_start(self):
+        self.core_copy().start()
+
+    def core_wait(self):
+        self.core_copy().wait_recv()
+
+    def sent(self):
+        for j in range(self.at.sh.depth - 1):
+            self.z_copy(j).wait_send()
+        self.a_copy().wait_send()
+        self.b_copy(0).wait_send()
+        self.core_copy().wait_send()
+
+    def step(self, stage):
+        if stage == 0:
+            self.z_start()
+        elif stage == 1:
+            self.z_wait()
+            self.a_start()
+        elif stage == 2:
+            self.a_wait()
+            self.b_start()
+        elif stage == 3:
+            self.b_wait()
+            self.core_start()
+        else:
+            self.core_wait()
+
+
+def enter(at):
+    sh = at.sh
+    partners = [at.sibling(), at.x_peer(), at.y_peer(), at.ring(1), at.ring(-1)]
+    partners += [at.z_peer(j) for j in range(sh.depth - 1)]
+    barrier = pltpu.get_barrier_semaphore()
+    for partner in partners:
+        pl.semaphore_signal(barrier, inc=1, device_id=partner, device_id_type=MESH)
+    pl.semaphore_wait(barrier, len(partners))
+
+
+def slab(p, segs):
+    return pl.ds(pl.multiple_of(p * segs, segs), segs)
+
+
+def to_position_major(sh, stage, lanes, dest):
+    tiles = sh.width // 128
+    for j in range(tiles):
+        lanes[j] = stage[:, j * 128 : (j + 1) * 128].astype(f32)
+
+    def move(p, _):
+        for j in range(tiles):
+            both_stretches = [
+                lanes[j, pl.ds(p + st * sh.span, sh.groups, stride=sh.stretches * sh.span), :]
+                for st in range(sh.stretches)
+            ]
+            dest[slab(p, sh.segs), j * 128 : (j + 1) * 128] = jnp.concatenate(
+                both_stretches, 0
+            ).astype(dest.dtype)
+        return 0
+
+    lax.fori_loop(0, sh.span, move, 0)
+
+
+def wrap_before(sh, at, got):
+    half = sh.groups
+    wrapped = jnp.concatenate([jnp.zeros((half, sh.width), f32), got[:half]], 0)
+    return jnp.where(at.s == 0, wrapped, got)
+
+
+def wrap_after(sh, at, got):
+    half = sh.groups
+    wrapped = jnp.concatenate([got[half:], jnp.zeros((half, sh.width), f32)], 0)
+    return jnp.where(at.s == sh.count - 1, wrapped, got)
+
+
+def decay_over(rate, positions):
+    return jnp.exp(-positions * rate)
+
+
+class Exchange:
+    def __init__(self, sh, at, planes, xy, zs, sems):
+        self.sh, self.at, self.planes = sh, at, planes
+        self.xy, self.zs, self.sems = xy, zs, sems
+
+    def x_copy(self):
+        return send(self.xy.at[0], self.xy.at[1], self.sems, 0, self.at.x_peer())
+
+    def y_copy(self):
+        return send(self.xy.at[2], self.xy.at[3], self.sems, 1, self.at.y_peer())
+
+    def z_copy(self, j):
+        return send(self.xy.at[4], self.zs.at[j], self.sems, 2 + j, self.at.z_peer(j))
+
+    def sent(self):
+        self.x_copy().wait_send()
+        self.y_copy().wait_send()
+        for j in range(self.sh.depth - 1):
+            self.z_copy(j).wait_send()
+
+
+class Forward(Exchange):
+    def start(self, totals):
+        for i, part in enumerate(totals):
+            self.xy[0, i] = part
+        self.x_copy().start()
+
+    def after_x(self, rate):
+        sh, at = self.sh, self.at
+        self.x_copy().wait_recv()
+        fade = decay_over(rate, float(sh.span))
+        for i in range(2):
+            own, other = self.xy[0, i], self.xy[1, i]
+            first = jnp.where(at.x == 0, own, other)
+            second = jnp.where(at.x == 0, other, own)
+            self.xy[2, i] = fade * first + second
+        self.y_copy().start()
+
+    def after_y(self, rate):
+        sh, at = self.sh, self.at
+        self.y_copy().wait_recv()
+        fade = decay_over(rate, 2.0 * sh.span)
+        for i in range(2):
+            own, other = self.xy[2, i], self.xy[3, i]
+            first = jnp.where(at.y == 0, own, other)
+            second = jnp.where(at.y == 0, other, own)
+            self.xy[4, i] = fade * first + second
+        for j in range(sh.depth - 1):
+            self.z_copy(j).start()
+
+    def after_z(self, rate, carry, total):
+        sh, at = self.sh, self.at
+        for j in range(sh.depth - 1):
+            self.z_copy(j).wait_recv()
+        plane = 4.0 * sh.span
+        z = at.z.astype(f32)
+        within = (2 * at.y + at.x).astype(f32) * sh.span
+        x_span = at.x.astype(f32) * sh.span
+        for i in range(2):
+            every = decay_over(rate, (sh.depth - 1.0 - z) * plane) * self.xy[4, i]
+            before = jnp.zeros_like(every)
+            for j in range(sh.depth - 1):
+                other = at.z_from(j)
+                o = other.astype(f32)
+                got = self.zs[j, i]
+                gap = jnp.maximum(z - 1.0 - o, 0.0) * plane
+                before += jnp.where(other < at.z, decay_over(rate, gap), 0.0) * got
+                every += decay_over(rate, (sh.depth - 1.0 - o) * plane) * got
+            state = decay_over(rate, within) * before
+            state += jnp.where(at.y == 1, decay_over(rate, x_span), 0.0) * self.xy[3, i]
+            state += jnp.where(at.x == 1, 1.0, 0.0) * self.xy[1, i]
+            half = sh.groups
+            earlier = decay_over(rate, z * plane + within) * every[:half]
+            carry[i] = state + jnp.concatenate([jnp.zeros_like(earlier), earlier], 0)
+            total[i] = every
+
+
+class Tops(Exchange):
+    def start(self, own):
+        self.xy[0, 0] = own
+        self.x_copy().start()
+
+    def after_x(self, rate):
+        sh, at = self.sh, self.at
+        self.x_copy().wait_recv()
+        own, other = self.xy[0, 0], self.xy[1, 0]
+        first = jnp.where(at.x == 0, own, other)
+        second = jnp.where(at.x == 0, other, own)
+        self.xy[2, 0] = jnp.maximum(first - sh.span * rate, second)
+        self.y_copy().start()
+
+    def after_y(self, rate):
+        sh, at = self.sh, self.at
+        self.y_copy().wait_recv()
+        own, other = self.xy[2, 0], self.xy[3, 0]
+        first = jnp.where(at.y == 0, own, other)
+        second = jnp.where(at.y == 0, other, own)
+        self.xy[4, 0] = jnp.maximum(first - 2.0 * sh.span * rate, second)
+        for j in range(sh.depth - 1):
+            self.z_copy(j).start()
+
+    def after_z(self, rate):
+        sh, at = self.sh, self.at
+        for j in range(sh.depth - 1):
+            self.z_copy(j).wait_recv()
+        plane = 4.0 * sh.span
+        most = self.xy[4, 0] - (sh.depth - 1.0 - at.z.astype(f32)) * plane * rate
+        for j in range(sh.depth - 1):
+            gap = (sh.depth - 1.0 - at.z_from(j).astype(f32)) * plane
+            most = jnp.maximum(most, self.zs[j, 0] - gap * rate)
+        half = sh.groups
+        return jnp.maximum(most[:half] - float(sh.count * sh.span) * rate, most[half:])
+
+
+def forward_kernel(
+    sh,
+    tok_hbm, cot_hbm, pack_ref,
+    w_out, vec_out, xp_out, cotp_out, k_out, v_out, gate_out, num_out, den_out, res_out, hin_out,
+    sin_out, s2_out, rg_out, gated_out, keyin_out, valin_out, gatin_out, final_out,
+    w, vall, vecs, got_pack, stage, lanes, xp, cotp, halo, halo32,
+    key_in, value_in, gate_in, k, v, gate, num, den, gated, res, hin, sin, s2, rg,
+    st_xy, st_z, top_xy, top_z, carry, total, finals,
+    local_sem, park_sem, pack_sems, ag_send, ag_recv, st_send, st_recv, top_send, top_recv,
+    halo_send, halo_recv,
+):
+    at = Place(sh)
+    segs, span, rows, half = sh.segs, sh.span, sh.rows, sh.half
+    mine, theirs = at.columns(at.r), at.columns(1 - at.r)
+    ag = (ag_send, ag_recv)
+    gathers = [Gather(at, w, (pl.ds(a, b - a),), ag, g) for g, (a, b) in enumerate(GROUPS)]
+    gather_v = Gather(at, vall, (), ag, len(GROUPS))
+
+    load_tok = pltpu.make_async_copy(tok_hbm, stage, local_sem.at[0])
+    load_tok.start()
+    enter(at)
+    pack_copy = send(
+        pack_ref.at[:, :, theirs], got_pack, (pack_sems.at[0], pack_sems.at[1]), 0, at.sibling()
+    )
+    pack_copy.start()
+    load_tok.wait()
+    to_position_major(sh, stage, lanes, xp)
+    halo_x = send(xp.at[pl.ds(rows - segs, segs)], halo.at[0], (halo_send, halo_recv), 0, at.ring(1))
+    halo_x.start()
+    load_cot = pltpu.make_async_copy(cot_hbm, stage, local_sem.at[1])
+    load_cot.start()
+
+    pack_copy.wait_recv()
+    for m in range(sh.mats):
+        own = pack_ref[m, : sh.own, mine].astype(f32)
+        other = got_pack[m, : sh.own].astype(f32)
+        first = jnp.where(at.r == 0, own, other)
+        second = jnp.where(at.r == 0, other, own)
+        w[m, at.z, at.y, at.x, :, mine] = jnp.concatenate([first, second], 0).astype(bf16)
+    vall[at.z, at.y, at.x, :, mine] = (
+        pack_ref[sh.mats, :16, mine].astype(f32) + got_pack[sh.mats, :16].astype(f32)
+    ).astype(bf16)
+    gather_v.step(0)
+    gathers[0].step(0)
+    gathers[1].step(0)
+    load_cot.wait()
+    to_position_major(sh, stage, lanes, cotp)
+    gather_v.step(1)
+    gathers[0].step(1)
+    gathers[2].step(0)
+    gather_v.step(2)
+    gathers[0].step(2)
+    gathers[1].step(1)
+    gathers[3].step(0)
+    gather_v.step(3)
+    gather_v.step(4)
+    spread = jnp.zeros((16, sh.width), f32)
+    for z in range(sh.depth):
+        for i in range(4):
+            spread += vall[z, i // 2, i % 2].astype(f32)
+    vecs[...] = spread
+
+    def vec(i):
+        return vecs[i : i + 1, :]
+
+    halo_x.wait_recv()
+    got, _ = normalise(halo[0].astype(f32))
+    got = wrap_before(sh, at, got * vec(MIXER_G) + vec(MIXER_B))
+
+    def blend_one(p, before):
+        here = slab(p, segs)
+        n1, _ = normalise(xp[here, :].astype(f32))
+        one = n1 * vec(MIXER_G) + vec(MIXER_B)
+        step = one - before
+        key_in[here, :] = (before + step * vec(KEY_SHARE)).astype(bf16)
+        value_in[here, :] = (before + step * vec(VALUE_SHARE)).astype(bf16)
+        gate_in[here, :] = (before + step * vec(GATE_SHARE)).astype(bf16)
+        return one
+
+    lax.fori_loop(0, span, blend_one, got)
+
+    gathers[0].step(3)
+    gathers[1].step(2)
+    gathers[2].step(1)
+    gathers[4].step(0)
+    gathers[0].step(4)
+
+    def matrix(m):
+        return w[m].reshape(sh.width, sh.width)
+
+    k[...] = dot(key_in[...], matrix(KEY)).astype(bf16)
+    v[...] = dot(value_in[...], matrix(VALUE)).astype(bf16)
+
+    rate = jnp.exp(vec(DECAY))
+    keep = jnp.exp(-rate)
+    zero = jnp.zeros((segs, sh.width), f32)
+
+    def add_up(p, state):
+        a, b, top = state
+        here = slab(p, segs)
+        key = k[here, :].astype(f32)
+        grown = jnp.exp(key)
+        top = jnp.maximum(top - rate, key)
+        return keep * a + grown * v[here, :].astype(f32), keep * b + grown, top
+
+    sum_num, sum_den, top = lax.fori_loop(
+        0, span, add_up, (zero, zero, jnp.full((segs, sh.width), -jnp.inf, f32))
+    )
+    states = Forward(sh, at, 2, st_xy, st_z, (st_send, st_recv))
+    states.start((sum_num, sum_den))
+    tops = Tops(sh, at, 1, top_xy, top_z, (top_send, top_recv))
+    tops.start(top)
+
+    gathers[1].step(3)
+    gathers[2].step(2)
+    gathers[3].step(1)
+    gathers[5].step(0)
+    states.after_x(rate)
+    gathers[1].step(4)
+    gate[...] = sigmoid(dot(gate_in[...], matrix(GATE)))
+    states.after_y(rate)
+    tops.after_x(rate)
+    gathers[2].step(3)
+    gathers[3].step(2)
+    gathers[4].step(1)
+    states.after_z(rate, carry, total)
+    tops.after_y(rate)
+
+    boost_rate = jnp.exp(vec(FIRST))
+
+    def recur(p, state):
+        a, b = state
+        here = slab(p, segs)
+        grown = jnp.exp(k[here, :].astype(f32))
+        value = v[here, :].astype(f32)
+        boost = grown * boost_rate
+        num[here, :] = a
+        den[here, :] = b
+        mix = ((a + boost * value) / (b + boost)).astype(bf16).astype(f32)
+        gated[here, :] = (gate[here, :] * mix).astype(bf16)
+        return keep * a + grown * value, keep * b + grown
+
+    lax.fori_loop(0, span, recur, (carry[0], carry[1]))
+    res[...] = xp[...].astype(f32) + dot(gated[...], matrix(OUTPUT))
+
+    last = pl.ds(rows - segs, segs)
+    n2, _ = normalise(res[last, :])
+    halo32[0] = n2 * vec(CHANNEL_G) + vec(CHANNEL_B)
+    halo_two = send(halo32.at[0], halo32.at[1], (halo_send, halo_recv), 1, at.ring(1))
+    halo_two.start()
+    gathers[3].step(3)
+    gathers[4].step(2)
+    gathers[5].step(1)
+    final_top = tops.after_z(rate)
+    far = decay_over(rate, float(sh.count * span))
+    scale = jnp.exp(-final_top)
+    for i in range(2):
+        finals[i] = (far * total[i, : sh.groups] + total[i, sh.groups :]) * scale
+    finals[2] = final_top
+    halo_two.wait_recv()
+    got = wrap_before(sh, at, halo32[1])
+
+    def blend_two(p, before):
+        here = slab(p, segs)
+        n2, _ = normalise(res[here, :])
+        two = n2 * vec(CHANNEL_G) + vec(CHANNEL_B)
+        step = two - before
+        hin[here, :] = (before + step * vec(HIDDEN_SHARE)).astype(bf16)
+        sin[here, :] = (before + step * vec(SCREEN_SHARE)).astype(bf16)
+        return two
+
+    lax.fori_loop(0, span, blend_two, got)
+    s2[...] = sigmoid(dot(sin[...], matrix(SCREEN)))
+    rg[...] = (cotp[...].astype(f32) * s2[...]).astype(bf16)
+
+    gathers[2].step(4)
+    gathers[4].step(3)
+    gathers[5].step(2)
+    gathers[3].step(4)
+    gathers[5].step(3)
+    gathers[4].step(4)
+    gathers[5].step(4)
+    parks = [
+        (w, w_out), (vecs, vec_out), (xp, xp_out), (cotp, cotp_out), (k, k_out), (v, v_out),
+        (gate, gate_out), (num, num_out), (den, den_out), (res, res_out), (hin, hin_out),
+        (sin, sin_out), (s2, s2_out), (rg, rg_out), (gated, gated_out), (key_in, keyin_out),
+        (value_in, valin_out), (gate_in, gatin_out), (finals, final_out),
+    ]
+    copies = [pltpu.make_async_copy(a, b, park_sem.at[i]) for i, (a, b) in enumerate(parks)]
+    for c in copies:
+        c.start()
+    pack_copy.wait_send()
+    halo_x.wait_send()
+    halo_two.wait_send()
+    for g in gathers + [gather_v]:
+        g.sent()
+    states.sent()
+    tops.sent()
+    for c in copies:
+        c.wait()
+
+
+def forward(sh, tokens, cotangent, pack):
+    R, D, S, Z = sh.rows, sh.width, sh.segs, sh.depth
+    shape = jax.ShapeDtypeStruct
+    narrow, wide = ((R, D), bf16), ((R, D), f32)
+    w_shape = (sh.mats, Z, 2, 2, sh.chip, D)
+    outs = [
+        (w_shape, bf16), ((16, D), f32), narrow, narrow, narrow, narrow, wide, wide, wide, wide,
+        narrow, narrow, wide, narrow, narrow, narrow, narrow, narrow, ((3, sh.groups, D), f32),
+    ]
+    V = pltpu.VMEM
+    dma = pltpu.SemaphoreType.DMA
+    scratch = [
+        V(w_shape, bf16), V((Z, 2, 2, 16, D), bf16), V((16, D), f32),
+        V((sh.mats + 1, 32, sh.half), bf16), V((R, D), bf16), V((D // 128, R, 128), f32),
+        V(*narrow), V(*narrow), V((1, S, D), bf16), V((2, S, D), f32),
+        V(*narrow), V(*narrow), V(*narrow), V(*narrow), V(*narrow), V(*wide), V(*wide), V(*wide),
+        V(*narrow), V(*wide), V(*narrow), V(*narrow), V(*wide), V(*narrow),
+        V((5, 2, S, D), f32), V((Z - 1, 2, S, D), f32), V((5, 1, S, D), f32),
+        V((Z - 1, 1, S, D), f32), V((2, S, D), f32), V((2, S, D), f32), V((3, sh.groups, D), f32),
+        dma((2,)), dma((len(outs),)), dma((2, 1)), dma((len(GROUPS) + 1, Z + 2)),
+        dma((len(GROUPS) + 1, Z + 2)), dma((Z + 1,)), dma((Z + 1,)), dma((Z + 1,)), dma((Z + 1,)),
+        dma((2,)), dma((2,)),
+    ]
+    anywhere = pl.BlockSpec(memory_space=pl.ANY)
+    return pl.pallas_call(
+        functools.partial(forward_kernel, sh),
+        out_shape=[shape(s, t) for s, t in outs],
+        in_specs=[anywhere, anywhere, pl.BlockSpec(memory_space=pltpu.VMEM)],
+        out_specs=[anywhere] * len(outs),
+        scratch_shapes=scratch,
+        compiler_params=pltpu.CompilerParams(
+            collective_id=0, has_side_effects=True, vmem_limit_bytes=60 * 2**20
+        ),
+    )(tokens.reshape(R, D), cotangent.reshape(R, D), pack)
+
+
+def mm(left, right):
+    return jnp.dot(left, right, preferred_element_type=f32)
+
+
+def mm_nt(left, right):
+    return lax.dot_general(left, right, (((1,), (1,)), ((), ())), preferred_element_type=f32)
+
+
+def mm_tn(left, right):
+    return lax.dot_general(left, right, (((0,), (0,)), ((), ())), preferred_element_type=f32)
 
 
 def ring(value, steps):
@@ -55,7 +644,7 @@
     return jnp.where(spot == count - 1, wrapped, pairs).reshape(got.shape)
 
 
-def forward_kernel(k_ref, v_ref, carry_ref, decay_ref, first_ref, num_ref, den_ref, mix_ref):
+def plain_scan(k_ref, v_ref, carry_ref, decay_ref, first_ref, num_ref, den_ref, mix_ref):
     keep = jnp.exp(-jnp.exp(decay_ref[...]))
     boost_rate = jnp.exp(first_ref[...])
 
@@ -72,7 +661,7 @@
     lax.fori_loop(0, k_ref.shape[0], step, (carry_ref[0], carry_ref[1]))
 
 
-def backward_kernel(
+def plain_scan_back(
     k_ref, v_ref, num_ref, den_ref, mix_ref, grad_ref, carry_ref, decay_ref, first_ref,
     kg_ref, vg_ref, first_grad_ref, decay_grad_ref,
 ):
@@ -112,7 +701,7 @@
     )(*operands)
 
 
-def body(
+def plain_body(
     tokens, mixer_gain, mixer_bias, key_blend, value_blend, gate_blend, time_decay, time_first,
     key_weight, value_weight, gate_weight, output_weight, channel_gain, channel_bias,
     hidden_blend, screen_blend, hidden_weight, screen_weight, return_weight, cotangent,
@@ -209,7 +798,7 @@
     final_den = own_slab(final[1]) * scaling
 
     num, den, mix_raw = call(
-        forward_kernel, [(cube, f32)] * 3, k.reshape(cube), v.reshape(cube), carry,
+        plain_scan, [(cube, f32)] * 3, k.reshape(cube), v.reshape(cube), carry,
         decay_log, first_log,
     )
     mix = mix_raw.reshape(rows, width).astype(bf16).astype(f32)
@@ -272,7 +861,7 @@
     carry = jnp.stack([carried_back(j * count + spot.astype(f32)) for j in range(stretches)], 2)
     carry = carry.reshape(2, segs, width)
     key_grad, value_grad, first_sum, decay_sum = call(
-        backward_kernel, [(cube, bf16)] * 2 + [((segs, width), f32)] * 2,
+        plain_scan_back, [(cube, bf16)] * 2 + [((segs, width), f32)] * 2,
         k.reshape(cube), v.reshape(cube), num, den, mix_raw, mix_grad.reshape(cube), carry,
         decay_log, first_log,
     )
@@ -341,6 +930,213 @@
     )
 
 
+def make_pack(sh, squares, hidden_weight, return_weight, vectors):
+    own, width, parts = sh.own, sh.width, sh.parts
+    owners = 2 * sh.count
+    hidden = hidden_weight.reshape(own, owners, parts, own)
+    hidden = jnp.transpose(hidden, (2, 0, 1, 3)).reshape(parts, own, width)
+    back = return_weight.reshape(parts, own, width)
+    both_parts = jnp.stack([hidden, back], 1).reshape(2 * parts, own, width)
+    mats = jnp.concatenate([jnp.stack(squares), both_parts], 0)
+    mats = jnp.pad(mats, ((0, 0), (0, 32 - own), (0, 0)))
+    place = (lax.axis_index("seq") * 2 + lax.axis_index("rep")) * own
+    tile = lax.dynamic_update_slice(
+        jnp.zeros((32, width), bf16), jnp.stack(vectors), (0, place)
+    )
+    return jnp.concatenate([mats, tile[None]], 0)
+
+
+def fused_body(sh, *args):
+    (
+        tokens, mixer_gain, mixer_bias, key_blend, value_blend, gate_blend, time_decay, time_first,
+        key_weight, value_weight, gate_weight, output_weight, channel_gain, channel_bias,
+        hidden_blend, screen_blend, hidden_weight, screen_weight, return_weight, cotangent,
+    ) = args
+    span, segs, width, own = sh.span, sh.segs, sh.width, sh.own
+    rows, groups, parts, inner = sh.rows, sh.groups, sh.parts, sh.inner
+    owners = 2 * sh.count
+    spot = lax.axis_index("seq")
+    vectors = (
+        mixer_gain, mixer_bias, key_blend, value_blend, gate_blend, time_decay, time_first,
+        channel_gain, channel_bias, hidden_blend, screen_blend,
+    )
+    squares = (key_weight, value_weight, gate_weight, output_weight, screen_weight)
+    pack = make_pack(sh, squares, hidden_weight, return_weight, vectors)
+    (
+        w, vecs, xp, cotp, k, v, gate, num, den, residual, hidden_in, screen_in, screen,
+        returned_grad, gated, key_in, value_in, gate_in, finals,
+    ) = forward(sh, tokens, cotangent, pack)
+    (
+        mixer_g, mixer_b, key_share, value_share, gate_share, decay_log, first_log,
+        channel_g, channel_b, hidden_share, screen_share,
+    ) = [vecs[i][None] for i in range(len(vectors))]
+    w = w.reshape(sh.mats, width, width)
+    w_key, w_value, w_gate, w_output, w_screen = [w[i] for i in range(5)]
+    w_hidden = jnp.concatenate([w[5 + 2 * c] for c in range(parts)], 1)
+    w_return = jnp.concatenate([w[6 + 2 * c] for c in range(parts)], 0)
+    cube = (span, segs, width)
+    rate = jnp.exp(decay_log)
+
+    def after(first):
+        got = ring(first, -1)
+        wrapped = jnp.concatenate([got[groups:], jnp.zeros_like(got[groups:])], 0)
+        return jnp.where(spot == sh.count - 1, wrapped, got)
+
+    def before_rows(last):
+        got = ring(last, 1)
+        wrapped = jnp.concatenate([jnp.zeros_like(got[:groups]), got[:groups]], 0)
+        return jnp.where(spot == 0, wrapped, got)
+
+    x = xp.astype(f32)
+    n1, inv1 = normalise(x)
+    one = n1 * mixer_g + mixer_b
+    spread_one = one - jnp.concatenate([before_rows(one[-segs:]), one[:-segs]], 0)
+    n2, inv2 = normalise(residual)
+    two = n2 * channel_g + channel_b
+    spread_two = two - jnp.concatenate([before_rows(two[-segs:]), two[:-segs]], 0)
+    cot = cotp.astype(f32)
+    relu = jnp.maximum(mm(hidden_in, w_hidden), 0.0)
+    act = jnp.square(relu).astype(bf16)
+    returned = mm(act, w_return)
+    output = (residual + screen * returned).astype(bf16)
+
+    screen_grad = (cot * returned * screen * (1.0 - screen)).astype(bf16)
+    hidden_grad = (mm_nt(returned_grad, w_return) * (2.0 * relu)).astype(bf16)
+    dw_return = mm_tn(act, returned_grad)
+    dw_hidden = mm_tn(hidden_in, hidden_grad)
+    dw_screen = mm_tn(screen_in, screen_grad)
+    hidden_back = mm_nt(hidden_grad, w_hidden)
+    screen_back = mm_nt(screen_grad, w_screen)
+    d_hidden_blend = jnp.sum(hidden_back * spread_two, 0)
+    d_screen_blend = jnp.sum(screen_back * spread_two, 0)
+    ahead = hidden_back * (1.0 - hidden_share) + screen_back * (1.0 - screen_share)
+    two_grad = (
+        hidden_back * hidden_share
+        + screen_back * screen_share
+        + jnp.concatenate([ahead[segs:], after(ahead[:segs])], 0)
+    )
+    d_channel_gain = jnp.sum(two_grad * n2, 0)
+    d_channel_bias = jnp.sum(two_grad, 0)
+    residual_grad = cot + norm_back(two_grad, n2, inv2, channel_g)
+    output_grad = residual_grad.astype(bf16)
+    dw_output = mm_tn(gated, output_grad)
+    gated_grad = mm_nt(output_grad, w_output)
+    mix_grad = (gated_grad * gate).astype(bf16)
+
+    num, den = num.reshape(cube), den.reshape(cube)
+    kw = k.reshape(cube).astype(f32)
+    vw = v.reshape(cube).astype(f32)
+    boost = jnp.exp(first_log + kw)
+    mix_raw = (num + boost * vw) / (den + boost)
+    mix = mix_raw.reshape(rows, width).astype(bf16).astype(f32)
+    gate_grad = (gated_grad * mix * gate * (1.0 - gate)).astype(bf16)
+    num_grad = mix_grad.reshape(cube).astype(f32) / (den + boost)
+    den_grad = -num_grad * mix_raw
+    offsets = jnp.arange(span, dtype=f32)[:, None, None]
+    fade = jnp.exp(-offsets * rate)
+    totals = jnp.stack([jnp.sum(fade * num_grad, 0), jnp.sum(fade * den_grad, 0)])
+    everyone = lax.all_gather(totals, "seq", axis=0)
+    everyone = everyone.reshape(sh.count, 2, 2, groups, width)
+    everyone = jnp.transpose(everyone, (2, 0, 1, 3, 4)).reshape(2 * sh.count, 2, groups, width)
+    order = jnp.arange(2 * sh.count, dtype=f32)
+
+    def carried_back(here):
+        gap = order[:, None] - here - 1.0
+        scale = jnp.where(gap >= 0, jnp.exp(-jnp.maximum(gap, 0.0) * (span * rate)), 0.0)
+        return jnp.sum(scale[:, None, None, :] * everyone, 0)
+
+    carry = jnp.stack([carried_back(j * sh.count + spot.astype(f32)) for j in range(2)], 1)
+    carry = carry.reshape(2, segs, width)
+    key_grad, value_grad, first_sum, decay_sum = call(
+        plain_scan_back, [(cube, bf16)] * 2 + [((segs, width), f32)] * 2,
+        k.reshape(cube), v.reshape(cube), num, den, mix_raw, mix_grad.reshape(cube), carry,
+        decay_log, first_log,
+    )
+    key_grad = key_grad.reshape(rows, width)
+    value_grad = value_grad.reshape(rows, width)
+    d_first = jnp.sum(first_sum, 0)
+    d_decay = -rate[0] * jnp.exp(-rate[0]) * jnp.sum(decay_sum, 0)
+    dw_key = mm_tn(key_in, key_grad)
+    dw_value = mm_tn(value_in, value_grad)
+    dw_gate = mm_tn(gate_in, gate_grad)
+    key_back = mm_nt(key_grad, w_key)
+    value_back = mm_nt(value_grad, w_value)
+    gate_back = mm_nt(gate_grad, w_gate)
+    d_key_blend = jnp.sum(key_back * spread_one, 0)
+    d_value_blend = jnp.sum(value_back * spread_one, 0)
+    d_gate_blend = jnp.sum(gate_back * spread_one, 0)
+    ahead = (
+        key_back * (1.0 - key_share)
+        + value_back * (1.0 - value_share)
+        + gate_back * (1.0 - gate_share)
+    )
+    one_grad = (
+        key_back * key_share
+        + value_back * value_share
+        + gate_back * gate_share
+        + jnp.concatenate([ahead[segs:], after(ahead[:segs])], 0)
+    )
+    d_mixer_gain = jnp.sum(one_grad * n1, 0)
+    d_mixer_bias = jnp.sum(one_grad, 0)
+    input_grad = residual_grad + norm_back(one_grad, n1, inv1, mixer_g)
+
+    grads = [dw_key, dw_value, dw_gate, dw_output, dw_screen]
+    for c in range(parts):
+        grads += [dw_hidden[:, c * width : (c + 1) * width], dw_return[c * width : (c + 1) * width]]
+    packed = jnp.concatenate([d.reshape(owners, own, width).astype(bf16) for d in grads], 1)
+    summed = lax.psum_scatter(packed, both, scatter_dimension=0).astype(f32)
+    summed = summed.reshape(sh.mats, own, width)
+    small = jnp.stack(
+        [
+            d_mixer_gain, d_mixer_bias, d_key_blend, d_value_blend, d_gate_blend, d_decay, d_first,
+            d_channel_gain, d_channel_bias, d_hidden_blend, d_screen_blend,
+        ]
+    )
+    small = lax.psum(small, both)
+    place = (spot * 2 + lax.axis_index("rep")) * own
+    small = lax.dynamic_slice_in_dim(small, place, own, 1)
+
+    def batch_major(a):
+        return jnp.transpose(a.reshape(span, 2, groups, width), (2, 1, 0, 3))
+
+    return (
+        batch_major(output),
+        batch_major(input_grad),
+        *own_finals(sh, finals),
+        *own_grads(sh, small, summed),
+    )
+
+
+def own_finals(sh, finals):
+    share = sh.width // sh.count
+    cut = lax.dynamic_slice_in_dim(finals, lax.axis_index("seq") * share, share, 2)
+    return [cut[i] for i in range(3)]
+
+
+def own_grads(sh, small, summed):
+    own, owners, parts, inner = sh.own, 2 * sh.count, sh.parts, sh.inner
+    hidden = summed[FIRST_PART::2].reshape(parts, own, owners, own)
+    hidden = jnp.transpose(hidden, (1, 2, 0, 3)).reshape(own, inner)
+    back = summed[FIRST_PART + 1 :: 2].reshape(parts * own, sh.width)
+    return (
+        *[small[i] for i in range(7)],
+        *[summed[i] for i in (KEY, VALUE, GATE, OUTPUT)],
+        *[small[i] for i in range(7, 11)],
+        hidden,
+        summed[SCREEN],
+        back,
+    )
+
+
+def body(*args):
+    tokens, hidden_weight = args[0], args[16]
+    groups, stretches, span, width = tokens.shape
+    sh = Shape(lax.axis_size("seq"), span, groups, stretches, width, hidden_weight.shape[1])
+    if lax.axis_size("rep") == 2 and sh.fits():
+        return fused_body(sh, *args)
+    return plain_body(*args)
+
+
 def solution(mesh):
     rows = P("rep", None, "seq", None)
     owned = P(both)

time: 614 us -> 541 us (0.88)
  Pallas kernels: 15.3 us -> 142 us
  local copies, waits for them, and re-layouts: 156 us -> 86.2 us
  waiting for transfers between devices: 159 us -> 114 us
  blocking collectives: 84.5 us -> 41.6 us
  other arithmetic: 57.3 us -> 33.2 us
  matrix products: 98.7 us -> 92 us
  starting transfers between devices: 18.7 us -> 12.1 us
    pallas_call x0 -> x1, Pallas kernels: none -> 133 us  [forward(): pl.pallas_call(functools.partial(forward_kernel, sh), out_shape=[shape(s,...]
    all_gather x1 -> x0, blocking collectives: 44.1 us -> none  [body(): spread_vectors = lax.all_gather(jnp.stack(vectors), both, axis=0)]
    convert_element_type x11 -> x0, local copies, waits for them, and re-layouts: 40.9 us -> none  [the longest x2 9.77 us: body(): cot = position_major(cotangent).astype(f32)]
    all_gather x3 -> x1, waiting for transfers between devices: 61.7 us -> 38 us  [fused_body(): everyone = lax.all_gather(totals, 'seq', axis=0)]
    reduce_scatter x1, waiting for transfers between devices: 94.3 us -> 76.4 us  [fused_body(): summed = lax.psum_scatter(packed, both, scatter_dimension=0).astype(f32)]
    reshape x19 -> x5, local copies, waits for them, and re-layouts: 28.3 us -> 12.5 us  [the longest x2 6.74 us: batch_major(): return jnp.transpose(a.reshape(span, 2, groups, width), (2, 1, 0, 3))]
    mul x12 -> x0, local copies, waits for them, and re-layouts: 12.3 us -> none  [the longest x1 1.39 us: body(): screen_in = (before + spread_two * screen_share).astype(bf16)]
    convert_element_type x6 -> x1, other arithmetic: 11.7 us -> 1.09 us  [fused_body(): summed = lax.psum_scatter(packed, both, scatter_dimension=0).astype(f32)]
  transfers between devices with their start and end apart: 8 -> 6, of which waited for: 5 -> 2; matrix products, arithmetic and copies ran while one was open for 27% -> 18% of each run, Pallas kernels for 0% -> 0%
where the time goes in v2:
time: 541 us; the launch traced here: 538 us
  Pallas kernels  142 us (26%)
  waiting for transfers between devices  114 us (21%)
  matrix products  92 us (17%)
  local copies, waits for them, and re-layouts  86.2 us (16%)
  blocking collectives  41.6 us (8%)
  other arithmetic  33.2 us (6%)
  between operations  15.6 us (3%)
  starting transfers between devices  12.1 us (2%)
    pallas_call x1, Pallas kernels, forward(): pl.pallas_call(functools.partial(forward_kernel, sh), out_shape=[shape(s,...  133 us
    reduce_scatter x1, waiting for transfers between devices, fused_body(): summed = lax.psum_scatter(packed, both, scatter_dimension=0).astype(f32)  76.4 us
    psum x1, blocking collectives, fused_body(): small = lax.psum(small, both)  41.6 us
    dot_general x7, matrix products, mm_nt(): lax.dot_general(left, right, (((1,), (1,)), ((), ())), preferred_element_...  41.4 us
    all_gather x1, waiting for transfers between devices, fused_body(): everyone = lax.all_gather(totals, 'seq', axis=0)  38 us
    unnamed x211, local copies, waits for them, and re-layouts  31.4 us
    dot_general x7, matrix products, mm_tn(): lax.dot_general(left, right, (((0,), (0,)), ((), ())), preferred_element_...  27 us
    dot_general x2, matrix products, mm(): return jnp.dot(left, right, preferred_element_type=f32)  23.6 us
  transfers between devices with their start and end apart: 6, of which 2 were waited for; matrix products, arithmetic and copies ran while one was open for 18% of the time, Pallas kernels for 0%

profile of v2, /device:TPU:0, one launch (start us, length us, event | category | flops | bytes accessed | tf_op | source)
XLA Modules:
  0.0 537.5 jit_solution(9672166760749736196)
XLA Ops:
  8.2 2.1 reshape.372
  10.5 1.2 stack_reshape.6
  13.8 132.5 %shard_map.371 = (bf16[13,4,2,2,48,768]{5,4,3,2,1,0:T(8,128)(2,1)}, f32[16,768]{1,0:T(8,128)}, bf16[1024,768]{1,0:T(8,128)(2,1)}, bf16[1024,768]{1,0:T(8,128)(2,...) custom-call(bf16[1024,768]{1,0:T(8,128)(2,1)} %bitcast.188, ...), custom_call_target="tpu_custom_call" | custom-call | tf_op jit(solution)/shard_map/pallas_call | solution.py:603
  146.3 1.8 slice_reduce_fusion
  148.1 2.1 reduce_sum.209
  150.8 9.8 %fusion.37 = (bf16[1,4,2,2,48,768]{5,4,3,2,1,0:T(8,128)(2,1)}, bf16[1,4,2,2,48,768]{5,4,3,2,1,0:T(8,128)(2,1)}, bf16[1,4,2,2,48,768]{5,4,3,2,1,0:T(8,128)(2,1)},...) fusion(bf16[13,4,2,2,48,768]{5,4,3,2,1,0:T(8,128)(2,1)} %get-tu, ...), kind=kLoop, calls=%fused_computation.162 | loop fusion | bytes 30670848 | tf_op jit(solution)/shard_map/slice | solution.py:974
  160.7 8.9 %fusion.22 = f32[1024,3072]{1,0:T(8,128)} fusion(bf16[1024,768]{1,0:T(8,128)(2,1)S(1)} %copy-done.95, bf16[768,768]{1,0:T(8,128)(2,1)S(1)} %bitcast.197, bf16[768,768]{1,0:T(8,128)(2,1)S(1)} %bitcast.199, bf16[768,768]{1,0:T(8,128)(2,1)S(1)} %bitcast.201, bf16[768,768]{1,0:T(8,128)(2,1)S(1)} %bitcast.203), kind=kOutput, calls=%fused_computation.69 | convolution fusion | flops 4850712576 | bytes 18874368 | tf_op jit(solution)/shard_map/dot_general | solution.py:616
  169.6 14.7 %fusion.15 = (bf16[1024,768]{1,0:T(8,128)(2,1)}, bf16[1024,768]{1,0:T(8,128)(2,1)}, f32[1024,768]{1,0:T(8,128)S(1)}) fusion(f32[1024,768]{1,0:T(8,128)} %get-tuple-element.47, bf16[1024,768]{1,0:T(8,128)(2,1)S(1)} %copy-done.36, f32[1024,768]{1,0:T(8,128)S(1)} %copy-done.3, f32[768]{0:T(1024)S(1)} %get-tuple-element.89, f32[768]{0:T(1024)S(1)} %get-tuple-element.103, ...), kind=kOutput, calls=%fused_computation.25 | convolution fusion | flops 4870373376 | bytes 31471616 | tf_op jit(solution)/shard_map/dot_general | solution.py:616
  184.3 1.7 copy-done.19
  186.0 5.8 %collective-permute-start.3 = (f32[16,768]{1,0:T(8,128)S(1)}, f32[16,768]{1,0:T(8,128)S(1)}, u32[]{:S(2)}, u32[]{:S(2)}) collective-permute-start(f32[16,768]{1,0:T(8,128)S(1)} %slice.315), channel_id=1, source_target_pairs={{0,2},{2,4},{4,6},{6,8},{8,10},{10,12},{12,14},{14,16},{16,18},{18... | collective-permute-start | bytes 147464 | tf_op jit(solution)/shard_map/ppermute | solution.py:629
  191.8 12.2 %multiply_convert_fusion = bf16[1024,3072]{1,0:T(8,128)(2,1)} fusion(f32[1024,3072]{1,0:T(8,128)} %fusion.22, bf16[1024,768]{1,0:T(8,128)(2,1)} %get-tuple-element.51, bf16[768,768]{1,0:T(8,128)(2,1)} %bitcast.206, bf16[768,768]{1,0:T(8,128)(2,1)} %bitcast.208, bf16[768,768]{1,0:T(8,128)(2,1)} %bitcast.210, bf16[768,768]{1,0:T(8,128)(2,1)} %bitcast.212), kind=kOutput, calls=%fused_computation | convolution fusion | flops 4863295488 | bytes 25165824 | tf_op jit(solution)/shard_map/dot_general | solution.py:620
  204.1 9.6 %fusion.21 = f32[1024,768]{1,0:T(8,128)} fusion(bf16[1024,3072]{1,0:T(8,128)(2,1)} %multiply_convert_fusion, bf16[768,768]{1,0:T(8,128)(2,1)S(1)} %bitcast.198, bf16[768,768]{1,0:T(8,128)(2,1)S(1)} %bitcast.200, bf16[768,768]{1,0:T(8,128)(2,1)S(1)} %bitcast.202, bf16[768,768]{1,0:T(8,128)(2,1)S(1)} %bitcast.204), kind=kOutput, calls=%fused_computation.68 | convolution fusion | flops 4850712576 | bytes 14155776 | tf_op jit(solution)/shard_map/dot_general | solution.py:620
  213.8 5.6 %convolution_convert_fusion.1 = bf16[768,3072]{1,0:T(8,128)(2,1)S(1)} fusion(bf16[1024,768]{1,0:T(8,128)(2,1)S(1)} %copy-done.96, bf16[1024,3072]{1,0:T(8,128)(2,1)S(1)} %copy-done.97), kind=kOutput, calls=%fused_computation.3 | convolution fusion | flops 4834197504 | bytes 12582912 | tf_op jit(solution)/shard_map/dot_general | solution.py:624
  219.4 2.5 fusion.39
  221.9 1.5 copy-done.7
  224.8 2.7 add_divide_fusion.mix_ref
  228.2 1.8 slice.317
  230.1 8.5 %multiply_reduce_fusion = (f32[768]{0:T(1024)}, f32[768]{0:T(1024)}, f32[1024,768]{1,0:T(8,128)S(1)}, f32[1024,768]{1,0:T(8,128)}) fusion(f32[1024,768]{1,0:T(8,128)} %copy-done.19, f32[1008,768]{1,0:T(8,128)} %slice.317, f32[16,768]{1,0:T(8,128)S(1)} %pad_select_fusion, f32[1024,768]{1,0:T(8,128)} %fusion.21, f32[768]{0:T(1024)S(1)} %get-tuple-element.94, ...), kind=kOutput, calls=%fused_computation.31 | convolution fusion | flops 1215035904 | bytes 18493440 | tf_op jit(solution)/shard_map/dot_general | solution.py:620
  238.6 1.6 copy-done.16
  241.8 2.6 copy.61
  244.4 2.6 copy.62
  247.0 2.2 slice.306
  249.3 1.3 slice.308
  251.4 4.7 multiply_reduce_fusion.2
  256.1 1.3 convert_add_fusion
  258.0 2.1 copy-done.15
  261.3 3.6 multiply_convert_fusion.2
  264.9 1.5 multiply_reduce_fusion.7
  267.1 8.9 %convolution_convert_fusion = bf16[3072,768]{1,0:T(8,128)(2,1)S(1)} fusion(bf16[1024,768]{1,0:T(8,128)(2,1)} %get-tuple-element.51, f32[1024,3072]{1,0:T(8,128)} %fusion.22), kind=kOutput, calls=%fused_computation.2 | convolution fusion | flops 4843634688 | bytes 18874368 | tf_op jit(solution)/shard_map/dot_general | solution.py:624
  276.1 2.5 fusion.38
  279.7 2.5 convolution_convert_fusion.2
  282.2 2.5 convolution_convert_fusion.4
  284.7 2.5 convolution_convert_fusion.3
  287.2 38.0 %all-gather.3.cloned.1.call-done = f32[32,16,768]{2,1,0:T(8,128)} async-done(((f32[2,16,768]{2,1,0:T(8,128)}), f32[32,16,768]{2,1,0:T(8,128)}) %all-gather.3.cloned.1.call-update) | async-done | bytes 1572880 | tf_op jit(solution)/shard_map/all_gather | solution.py:1038
  325.2 1.7 multiply_reduce_fusion.13
  326.9 9.8 %shard_map.372 = (bf16[64,16,768]{2,1,0:T(8,128)(2,1)S(1)}, bf16[64,16,768]{2,1,0:T(8,128)(2,1)S(1)}, f32[16,768]{1,0:T(8,128)S(1)}, f32[16,768]{1,0:T(8,128)S(1)}) custom-call(bf16[64,16,768]{2,1,0:T(8,128)(2,1)S(1)} %bitcast.153, bf16[64,16,768]{2,1,0:T(8,128)(2,1)} %bitcast.164, f32[64,16,768]{2,1,0:T(8,128)} %bitcast.161, f32[64,16,768]{2,1,0:T(8,128)} %bitcast.158, ...), custom_call_target="tpu_custom_call" | custom-call | tf_op jit(solution)/shard_map/pallas_call | solution.py:695
  336.8 2.4 fusion.19
  339.2 2.5 fusion.18
  341.7 1.2 constant_dynamic-update-slice_fusion.16
  346.3 1.1 constant_dynamic-update-slice_fusion.12
  349.7 1.2 constant_dynamic-update-slice_fusion.9
  350.9 1.2 constant_dynamic-update-slice_fusion.8
  352.1 1.2 constant_dynamic-update-slice_fusion.7
  353.3 1.1 constant_dynamic-update-slice_fusion.6
  354.5 1.4 copy-done.5
  357.4 1.6 copy-done.10
  359.0 1.4 collective-permute-start.2
  360.5 1.4 dynamic-slice_bitcast_fusion
  361.9 4.0 slice.314
  365.9 3.3 copy.67
  369.3 2.9 fusion.41
  372.3 1.4 fusion.42
  374.6 1.9 copy-done.35
  376.4 3.2 multiply_add_fusion.1
  379.6 1.8 copy-done.17
  381.4 4.1 collective-permute-start.1
  386.3 4.0 slice.309
  390.4 9.0 %fusion.10 = (f32[768]{0:T(1024)S(1)}, f32[1024]{0:T(1024)S(1)}, f32[1024]{0:T(1024)S(1)}, f32[768]{0:T(1024)S(1)}, f32[768]{0:T(1024)S(1)}, /*index=5*/f32[768]...) fusion(bf16[1024,768]{1,0:T(8,128)(2,1)S(1)} %copy-done.6, f32[1024]{0:T(1024)S(1)} %add_rsqrt_fusion, ...), kind=kLoop, calls=%fused_computation.20 | loop fusion | flops 21227776 | bytes 20494336 | tf_op jit(solution)/shard_map/reduce_sum | solution.py:1079
  399.5 1.2 fusion.9
  400.7 3.5 copy.66
  404.3 41.6 %psum.7 = f32[11,768]{1,0:T(8,128)S(1)} all-reduce(f32[11,768]{1,0:T(8,128)S(1)} %stack.140), channel_id=1, replica_groups=mesh['seq'=16,'rep'=2] {'seq','rep'}, use_global_device_ids=true, to_apply=%region_23.24 | all-reduce | flops 8448 | bytes 67584 | tf_op jit(solution)/shard_map/psum | solution.py:1095
  446.6 76.4 %reduce-scatter.2.cloned.1.call-done = bf16[1,312,768]{2,1,0:T(8,128)(2,1)} async-done(((bf16[32,312,768]{2,1,0:T(8,128)(2,1)}), bf16[1,312,768]{2,1,0:T(8,128)(2,1)}) %reduce-scatter.2.cloned.1.call-update) | async-done | bytes 479248 | tf_op jit(solution)/shard_map/reduce_scatter | solution.py:1087
  526.7 1.2 copy.63
  527.9 2.6 reshape.386
  (263 shorter events, 25.1 us)
Async XLA Ops:
  7.2 4.5 copy-start.54
  7.2 4.6 copy-start.61
  7.2 4.6 copy-start.62
  7.2 4.6 copy-start.63
  7.2 4.6 copy-start.64
  7.2 4.7 copy-start.80
  7.3 4.7 copy-start.81
  7.3 4.7 copy-start.82
  7.3 4.7 copy-start.83
  7.3 4.7 copy-start.84
  7.3 4.7 copy-start.85
  7.3 4.7 copy-start.86
  7.3 4.7 copy-start.87
  7.3 4.7 copy-start.88
  7.3 4.7 copy-start.89
  7.3 4.7 copy-start.90
  7.4 317.9 %all-gather.3.cloned.1.call-start = ((), (), s32[]{:S(2)}) async-start(), calls=%async_computation.2 | async-start | bytes 1671168 | tf_op jit(solution)/shard_map/all_gather | solution.py:1038
  148.1 21.4 %copy-start.57 = (f32[768]{0:T(1024)}, f32[768]{0:T(1024)S(1)}, u32[]{:S(2)}) copy-start(f32[768]{0:T(1024)S(1)} %get-tuple-element.103) | copy-start | bytes 9220
  148.1 73.8 %copy-start.59 = (f32[768]{0:T(1024)}, f32[768]{0:T(1024)S(1)}, u32[]{:S(2)}) copy-start(f32[768]{0:T(1024)S(1)} %get-tuple-element.92) | copy-start | bytes 9220
  150.8 18.8 %copy-start.55 = (f32[1024]{0:T(1024)}, f32[1024]{0:T(1024)S(1)}, u32[]{:S(2)}) copy-start(f32[1024]{0:T(1024)S(1)} %add_rsqrt_fusion.1) | copy-start | bytes 12292
  150.8 9.8 %copy-start.95 = (bf16[1024,768]{1,0:T(8,128)(2,1)S(1)}, bf16[1024,768]{1,0:T(8,128)(2,1)}, u32[]{:S(2)}) copy-start(bf16[1024,768]{1,0:T(8,128)(2,1)} %get-tuple-element.48) | copy-start | bytes 4718596
  160.6 9.0 %copy-start.46 = (bf16[1,4,2,2,48,768]{5,4,3,2,1,0:T(8,128)(2,1)}, bf16[1,4,2,2,48,768]{5,4,3,2,1,0:T(8,128)(2,1)S(1)}, u32[]{:S(2)}) copy-start(bf16[1,4,2,2,48,768]{5,4,3,2,1,0:T(8,128)(2,1)S(1)} %get-tuple-element.117) | copy-start | bytes 3538948
  160.6 9.0 %copy-start.48 = (bf16[1,4,2,2,48,768]{5,4,3,2,1,0:T(8,128)(2,1)}, bf16[1,4,2,2,48,768]{5,4,3,2,1,0:T(8,128)(2,1)S(1)}, u32[]{:S(2)}) copy-start(bf16[1,4,2,2,48,768]{5,4,3,2,1,0:T(8,128)(2,1)S(1)} %get-tuple-element.118) | copy-start | bytes 3538948
  160.6 8.9 %copy-start.50 = (bf16[1,4,2,2,48,768]{5,4,3,2,1,0:T(8,128)(2,1)}, bf16[1,4,2,2,48,768]{5,4,3,2,1,0:T(8,128)(2,1)S(1)}, u32[]{:S(2)}) copy-start(bf16[1,4,2,2,48,768]{5,4,3,2,1,0:T(8,128)(2,1)S(1)} %get-tuple-element.119) | copy-start | bytes 3538948
  160.6 8.9 %copy-start.52 = (bf16[1,4,2,2,48,768]{5,4,3,2,1,0:T(8,128)(2,1)}, bf16[1,4,2,2,48,768]{5,4,3,2,1,0:T(8,128)(2,1)S(1)}, u32[]{:S(2)}) copy-start(bf16[1,4,2,2,48,768]{5,4,3,2,1,0:T(8,128)(2,1)S(1)} %get-tuple-element.120) | copy-start | bytes 3538948
  160.6 8.9 %copy-start.36 = (bf16[1024,768]{1,0:T(8,128)(2,1)S(1)}, bf16[1024,768]{1,0:T(8,128)(2,1)}, u32[]{:S(2)}) copy-start(bf16[1024,768]{1,0:T(8,128)(2,1)} %get-tuple-element.50) | copy-start | bytes 4718596
  186.0 44.1 %collective-permute-start.3 = (f32[16,768]{1,0:T(8,128)S(1)}, f32[16,768]{1,0:T(8,128)S(1)}, u32[]{:S(2)}, u32[]{:S(2)}) collective-permute-start(f32[16,768]{1,0:T(8,128)S(1)} %slice.315), channel_id=1, source_target_pairs={{0,2},{2,4},{4,6},{6,8},{8,10},{10,12},{12,14},{14,16},{16,18},{18... | collective-permute-start | bytes 147464 | tf_op jit(solution)/shard_map/ppermute | solution.py:629
  191.8 12.3 %copy-start.47 = (bf16[1,4,2,2,48,768]{5,4,3,2,1,0:T(8,128)(2,1)S(1)}, bf16[1,4,2,2,48,768]{5,4,3,2,1,0:T(8,128)(2,1)}, u32[]{:S(2)}) copy-start(bf16[1,4,2,2,48,768]{5,4,3,2,1,0:T(8,128)(2,1)} %copy-done.46) | copy-start | bytes 3538948
  191.8 12.3 %copy-start.49 = (bf16[1,4,2,2,48,768]{5,4,3,2,1,0:T(8,128)(2,1)S(1)}, bf16[1,4,2,2,48,768]{5,4,3,2,1,0:T(8,128)(2,1)}, u32[]{:S(2)}) copy-start(bf16[1,4,2,2,48,768]{5,4,3,2,1,0:T(8,128)(2,1)} %copy-done.48) | copy-start | bytes 3538948
  191.8 12.3 %copy-start.51 = (bf16[1,4,2,2,48,768]{5,4,3,2,1,0:T(8,128)(2,1)S(1)}, bf16[1,4,2,2,48,768]{5,4,3,2,1,0:T(8,128)(2,1)}, u32[]{:S(2)}) copy-start(bf16[1,4,2,2,48,768]{5,4,3,2,1,0:T(8,128)(2,1)} %copy-done.50) | copy-start | bytes 3538948
  191.8 12.3 %copy-start.53 = (bf16[1,4,2,2,48,768]{5,4,3,2,1,0:T(8,128)(2,1)S(1)}, bf16[1,4,2,2,48,768]{5,4,3,2,1,0:T(8,128)(2,1)}, u32[]{:S(2)}) copy-start(bf16[1,4,2,2,48,768]{5,4,3,2,1,0:T(8,128)(2,1)} %copy-done.52) | copy-start | bytes 3538948
  204.1 9.7 %copy-start.96 = (bf16[1024,768]{1,0:T(8,128)(2,1)S(1)}, bf16[1024,768]{1,0:T(8,128)(2,1)}, u32[]{:S(2)}) copy-start(bf16[1024,768]{1,0:T(8,128)(2,1)} %get-tuple-element.48) | copy-start | bytes 4718596
  204.1 9.7 %copy-start.97 = (bf16[1024,3072]{1,0:T(8,128)(2,1)S(1)}, bf16[1024,3072]{1,0:T(8,128)(2,1)}, u32[]{:S(2)}) copy-start(bf16[1024,3072]{1,0:T(8,128)(2,1)} %multiply_convert_fusion) | copy-start | bytes 18874372
  219.4 5.0 copy-start.14
  219.4 5.4 %copy-start.23 = (bf16[1024,768]{1,0:T(8,128)(2,1)S(1)}, bf16[1024,768]{1,0:T(8,128)(2,1)}, u32[]{:S(2)}) copy-start(bf16[1024,768]{1,0:T(8,128)(2,1)} %get-tuple-element.55) | copy-start | bytes 4718596
  230.1 11.6 %copy-start.70 = (f32[768]{0:T(1024)S(1)}, f32[768]{0:T(1024)}, u32[]{:S(2)}) copy-start(f32[768]{0:T(1024)} %get-tuple-element.91) | copy-start | bytes 9220
  230.1 11.6 %copy-start.79 = (f32[64]{0:T(128)S(1)}, f32[64]{0:T(128)}, u32[]{:S(2)}) copy-start(f32[64]{0:T(128)} %iota_negate_fusion) | copy-start | bytes 772
  240.9 8.4 %collective-permute-start = (f32[16,768]{1,0:T(8,128)}, f32[16,768]{1,0:T(8,128)}, u32[]{:S(2)}, u32[]{:S(2)}) collective-permute-start(f32[16,768]{1,0:T(8,128)} %slice.307), channel_id=1, source_target_pairs={{0,30},{2,0},{4,2},{6,4},{8,6},{10,8},{12,10},{14,12},{16,14},{18,... | collective-permute-start | bytes 147464 | tf_op jit(solution)/shard_map/ppermute | solution.py:629
  247.0 4.4 copy-start.4
  247.0 4.4 copy-start.18
  247.0 4.4 copy-start.56
  247.0 4.4 copy-start.58
  247.0 4.4 copy-start.68
  247.0 4.4 copy-start.69
  251.4 4.7 copy-start.37
  256.1 4.3 copy-start.45
  256.1 4.2 copy-start.60
  256.1 5.2 copy-start.91
  257.4 7.5 %copy-start.11 = (f32[1024,768]{1,0:T(8,128)}, f32[1024,768]{1,0:T(8,128)S(1)}, u32[]{:S(2)}) copy-start(f32[1024,768]{1,0:T(8,128)S(1)} %convert_add_fusion) | copy-start | bytes 9437188
  267.1 255.9 %reduce-scatter.2.cloned.1.call-start = ((), (), s32[]{:S(2)}) async-start(), calls=%async_computation.1 | async-start | bytes 15814656 | tf_op jit(solution)/shard_map/reduce_scatter | solution.py:1087
  326.9 9.8 %copy-start.38 = (bf16[768,1024]{1,0:T(8,128)(2,1)S(1)}, bf16[768,1024]{1,0:T(8,128)(2,1)}, u32[]{:S(2)}) copy-start(bf16[768,1024]{1,0:T(8,128)(2,1)} %copy.61) | copy-start | bytes 4718596
  359.0 10.2 %collective-permute-start.2 = (f32[16,768]{1,0:T(8,128)S(1)}, f32[16,768]{1,0:T(8,128)S(1)}, u32[]{:S(2)}, u32[]{:S(2)}) collective-permute-start(f32[16,768]{1,0:T(8,128)S(1)} %slice.312), channel_id=1, source_target_pairs={{0,2},{2,4},{4,6},{6,8},{8,10},{10,12},{12,14},{14,16},{16,18},{18... | collective-permute-start | bytes 147464 | tf_op jit(solution)/shard_map/ppermute | solution.py:629
  361.9 7.3 %copy-start.72 = (f32[768]{0:T(1024)S(1)}, f32[768]{0:T(1024)}, u32[]{:S(2)}) copy-start(f32[768]{0:T(1024)} %get-tuple-element.74) | copy-start | bytes 9220
  372.2 4.2 copy-start.35
  372.3 4.2 copy-start.76
  372.3 4.2 copy-start.77
  372.3 4.2 copy-start.78
  373.7 5.9 %copy-start.22 = (f32[1024,768]{1,0:T(8,128)}, f32[1024,768]{1,0:T(8,128)S(1)}, u32[]{:S(2)}) copy-start(f32[1024,768]{1,0:T(8,128)S(1)} %fusion.42) | copy-start | bytes 9437188
  381.4 9.0 %collective-permute-start.1 = (f32[16,768]{1,0:T(8,128)S(1)}, f32[16,768]{1,0:T(8,128)S(1)}, u32[]{:S(2)}, u32[]{:S(2)}) collective-permute-start(f32[16,768]{1,0:T(8,128)S(1)} %slice.310), channel_id=1, source_target_pairs={{0,30},{2,0},{4,2},{6,4},{8,6},{10,8},{12,10},{14,12},{16,14},{18,... | collective-permute-start | bytes 147464 | tf_op jit(solution)/shard_map/ppermute | solution.py:629
  386.2 4.2 copy-start.6
  386.2 4.2 copy-start.73
  386.2 4.2 copy-start.74
  386.2 4.1 copy-start.75
  390.4 9.1 %copy-start.13 = (f32[1024,768]{1,0:T(8,128)S(1)}, f32[1024,768]{1,0:T(8,128)}, u32[]{:S(2)}) copy-start(f32[1024,768]{1,0:T(8,128)} %copy-done.11) | copy-start | bytes 9437188
  (40 other events, 112.8 us)
Sparse Core Ops, SparseCore 0:
  267.2 57.9 all-gather.2
  354.6 168.3 reduce-scatter.1
